TPU v7x, 256 devices: a whole 4x4x8 slice. The times are simulated.
256 devices in a mesh: grp: 16 (over y, z_lo), dev: 16 (over z_hi, x, core).
Axes of the slice: x: 4, y: 4, z: 8 (z_hi: 2, z_lo: 4; z = z_hi * 4 + z_lo), core: 2. Of those that a mesh axis runs over, the one named last changes fastest.
Arguments:
- history: bfloat16 [16, 64, 1024], P('grp', 'dev'), may hold values from -6 to 6
- candidates: bfloat16 [16, 16384, 1024], P('grp', 'dev'), may hold values from -6 to 6
- score_grad: float32 [16, 16384], P('grp', 'dev'), may hold values from -0.03125 to 0.03125
- req_counts: int32 [16, 64], P('grp'), may hold values from 1 to 2000, 16384 in all within a row
- owner_slot: int32 [16, 64], P('grp'), may hold values from 0 to 63, each once within a row
- encoder_weight: bfloat16 [1024, 1024], replicated, may hold values from -0.1875 to 0.1875
- user_weight: bfloat16 [1024, 2048], replicated, may hold values from -0.1875 to 0.1875
- cand_weight: bfloat16 [1024, 2048], replicated, may hold values from -0.1875 to 0.1875
- hidden_bias: float32 [2048], replicated, may hold values from -3 to 3
- scorer_weight: float32 [2048], replicated, may hold values from -6 to 6
Outputs:
- cand_gradient: float32 [1024, 2048], P('grp', 'dev')
- user_gradient: float32 [1024, 2048], P('grp', 'dev')
- encoder_gradient: float32 [1024, 1024], P('grp', 'dev')
- scorer_gradient: float32 [2048], replicated
- bias_gradient: float32 [2048], replicated
- history_gradient: float32 [16, 64, 1024], P('grp', 'dev')
Inputs may be any that keep to these rules, and one draw needn't show every extreme that they name: `req_counts`: each request has 1 to 2000 candidates, the counts of a group sum to 16384, and one request of each group has exactly 2000. `owner_slot`: each group's map is a permutation: every owner slot holds one request, and slot s lies on the device of index s // 4 along dev.
All inputs are finite; a program needn't handle non-finite values.
Results may differ from a plain program's by a relative error of at most 0.0054.
Values may be sent and summed in bfloat16 or wider, within the bound.
A program may use at most 128 MiB of HBM per device.

v0:
```python
import jax
import jax.numpy as jnp
from jax import lax
from jax.sharding import PartitionSpec as P


def silu_parts(values):
    sigma = jax.nn.sigmoid(values)
    return (values * sigma, sigma * (1.0 + values * (1.0 - sigma)))


def contract_first(left, right, precision=None):
    return lax.dot_general(
        left,
        right,
        (((0,), (0,)), ((), ())),
        precision=precision,
        preferred_element_type=jnp.float32,
    )


def contract_last(left, right):
    return lax.dot_general(
        left, right, (((1,), (1,)), ((), ())), preferred_element_type=jnp.float32
    )


def local(
    history,
    candidates,
    score_grad,
    req_counts,
    owner_slot,
    encoder_weight,
    user_weight,
    cand_weight,
    hidden_bias,
    scorer_weight,
):
    highest = lax.Precision.HIGHEST
    history_rows = history[0]
    cand_rows = candidates[0]
    dscore = score_grad[0]
    counts_group = req_counts[0]
    slot_map = owner_slot[0]
    cand_count = cand_rows.shape[0]
    slot_total = counts_group.shape[0]
    dev_index = lax.axis_index("dev")
    enc_pre = jnp.dot(history_rows, encoder_weight, preferred_element_type=jnp.float32)
    enc_act, enc_slope = silu_parts(enc_pre)
    user_vec = (history_rows.astype(jnp.float32) + enc_act).astype(jnp.bfloat16)
    user_proj = jnp.dot(user_vec, user_weight, preferred_element_type=jnp.float32).astype(
        jnp.bfloat16
    )
    proj_all = lax.all_gather(user_proj, "dev", axis=0, tiled=True)
    req_ends = jnp.cumsum(counts_group)
    row_index = dev_index * cand_count + lax.iota(jnp.int32, cand_count)
    request_id = jnp.sum((req_ends[None, :] <= row_index[:, None]).astype(jnp.int32), axis=1)
    slot_iota = lax.iota(jnp.int32, slot_total)
    slot_id = jnp.sum(
        jnp.where(request_id[:, None] == slot_iota[None, :], slot_map[None, :], 0), axis=1
    )
    selector = (slot_id[None, :] == slot_iota[:, None]).astype(jnp.bfloat16)
    pre_act = (
        jnp.dot(cand_rows, cand_weight, preferred_element_type=jnp.float32)
        + contract_first(selector, proj_all)
        + hidden_bias[None, :]
    )
    hidden_act, hidden_slope = silu_parts(pre_act)
    pre_grad = dscore[:, None] * scorer_weight[None, :] * hidden_slope
    grad_half = pre_grad.astype(jnp.bfloat16)
    grad_part = jnp.dot(selector, grad_half, preferred_element_type=jnp.float32)
    slot_grad = lax.psum_scatter(grad_part, "dev", scatter_dimension=0, tiled=True)
    cand_term = contract_first(cand_rows, grad_half)
    scorer_term = jnp.sum(dscore[:, None] * hidden_act, axis=0)
    bias_term = jnp.sum(pre_grad, axis=0)
    scorer_gradient, bias_gradient = lax.psum((scorer_term, bias_term), ("grp", "dev"))
    user_grad = contract_last(slot_grad.astype(jnp.bfloat16), user_weight)
    enc_grad = (user_grad * enc_slope).astype(jnp.bfloat16)
    history_grad = user_grad + contract_last(enc_grad, encoder_weight)
    user_term = contract_first(user_vec.astype(jnp.float32), slot_grad, highest)
    enc_term = contract_first(history_rows, enc_grad)
    cand_cols_sum, user_cols_sum, enc_cols_sum = (
        lax.psum_scatter(cand_term, "dev", scatter_dimension=1, tiled=True),
        lax.psum_scatter(user_term, "dev", scatter_dimension=1, tiled=True),
        lax.psum_scatter(enc_term, "dev", scatter_dimension=1, tiled=True),
    )
    summed = (
        lax.psum_scatter(cand_cols_sum, "grp", scatter_dimension=0, tiled=True),
        lax.psum_scatter(user_cols_sum, "grp", scatter_dimension=0, tiled=True),
        lax.psum_scatter(enc_cols_sum, "grp", scatter_dimension=0, tiled=True),
    )
    return (summed[0], summed[1], summed[2], scorer_gradient, bias_gradient, history_grad[None])


def solution(mesh):
    in_specs = (
        P("grp", "dev", None),
        P("grp", "dev", None),
        P("grp", "dev"),
        P("grp", None),
        P("grp", None),
        P(),
        P(),
        P(),
        P(),
        P(),
    )
    out_specs = (P("grp", "dev"), P("grp", "dev"), P("grp", "dev"), P(), P(), P("grp", "dev", None))
    return jax.shard_map(local, mesh=mesh, in_specs=in_specs, out_specs=out_specs, check_vma=False)
```

profile of v0, /device:TPU:1, one launch (start us, length us, event | category | flops | bytes accessed | tf_op | source)
XLA Modules:
  0.0 882.4 jit_solution(12633886117831577925)
XLA Ops:
  7.2 0.0 copy-start
  7.2 0.0 all-reduce.4.cloned.1.call-start
  7.2 2.1 fusion.14
  9.4 2.9 fusion
  12.2 35.1 %all-gather = bf16[16,4,2048]{2,1,0:T(4,128)(2,1)S(1)} all-gather(bf16[1,4,2048]{2,1,0:T(4,128)(2,1)S(1)} %fusion), channel_id=1, replica_groups=mesh['grp'=16,'dev'=16] {'dev'}, dimensions={0}, use_global_device_ids=true | all-gather | bytes 278528 | tf_op jit(solution)/shard_map/all_gather | solution.py:55
  47.4 0.1 reshape.48
  47.5 0.1 copy.25
  47.6 0.1 reduce-window.8
  47.7 0.1 reduce
  47.8 0.0 copy-start.4
  47.8 0.0 copy-start.5
  47.8 0.0 copy-start.6
  47.8 0.0 copy-start.7
  47.8 6.3 fusion.2
  54.1 0.1 convert_reduce_fusion
  54.3 0.1 select_reduce_fusion
  54.4 5.8 fusion.18
  60.2 0.0 copy-start.8
  60.2 2.0 copy-done.1
  62.2 1.6 fusion.4
  63.8 0.0 all-reduce.4.cloned.1.call-update
  63.8 0.0 reduce-scatter.17.cloned.1.call-start
  63.9 0.6 dynamic-slice
  65.1 171.1 %all-reduce.4.cloned.1.call-done = f32[64,2048]{1,0:T(8,128)} async-done(((f32[64,2048]{1,0:T(8,128)}), f32[64,2048]{1,0:T(8,128)}) %all-reduce.4.cloned.1.call-update) | async-done | bytes 524304
  236.3 3.4 fusion.12
  239.7 2.7 convolution_bitcast_fusion.1
  242.4 0.0 reduce-scatter.17.cloned.1.call-update
  242.4 0.0 reduce-scatter.11.cloned.1.call-start
  242.5 9.1 %convolution_bitcast_fusion = f32[1024,2048]{0,1:T(8,128)} fusion(bf16[1,1024,1024]{2,1,0:T(8,128)(2,1)S(1)} %copy-done, bf16[1024,2048]{1,0:T(8,128)(2,1)} %copy-done.1), kind=kOutput, calls=%fused_computation.4 | convolution fusion | flops 4294967296 | bytes 14680064 | tf_op jit(solution)/shard_map/dot_general | solution.py:13
  251.5 0.0 reduce-scatter.11.cloned.1.call-update
  251.6 0.0 reduce-scatter.13.cloned.1.call-start
  251.6 6.6 fusion.10
  258.2 0.0 reduce-scatter.13.cloned.1.call-update
  258.2 0.0 reduce-scatter.21.cloned.1.call-start
  258.2 88.0 %reduce-scatter.17.cloned.1.call-done = f32[1024,64]{0,1:T(8,128)} async-done(((f32[1024,1024]{0,1:T(8,128)}), f32[1024,64]{0,1:T(8,128)}) %reduce-scatter.17.cloned.1.call-update) | async-done | bytes 262160 | tf_op jit(solution)/shard_map/reduce_scatter | solution.py:86
  346.2 1.9 copy.30
  348.2 0.0 reduce-scatter.21.cloned.1.call-update
  348.2 0.0 reduce-scatter.19.cloned.1.call-start
  348.2 141.9 %reduce-scatter.11.cloned.1.call-done = f32[1024,128]{0,1:T(8,128)} async-done(((f32[1024,2048]{0,1:T(8,128)}), f32[1024,128]{0,1:T(8,128)}) %reduce-scatter.11.cloned.1.call-update) | async-done | bytes 524304 | tf_op jit(solution)/shard_map/reduce_scatter | solution.py:84
  490.1 2.1 copy.28
  492.2 0.0 reduce-scatter.19.cloned.1.call-update
  492.2 0.0 reduce-scatter.15.cloned.1.call-start
  492.2 141.4 %reduce-scatter.13.cloned.1.call-done = f32[1024,128]{1,0:T(8,128)} async-done(((f32[1024,2048]{1,0:T(8,128)}), f32[1024,128]{1,0:T(8,128)}) %reduce-scatter.13.cloned.1.call-update) | async-done | bytes 524304 | tf_op jit(solution)/shard_map/reduce_scatter | solution.py:85
  633.6 0.0 reduce-scatter.15.cloned.1.call-update
  633.6 75.3 %all-reduce.1 = (f32[2048]{0:T(1024)}, f32[2048]{0:T(1024)}) all-reduce(f32[2048]{0:T(1024)S(1)} %get-tuple-element.34, f32[2048]{0:T(1024)S(1)} %get-tuple-element.32), channel_id=1, replica_groups=mesh['grp'=16,'dev'=16] {'grp','dev'}, use_global_device_ids=true, to_apply=%region_11.12 | all-reduce | flops 4096 | bytes 32768 | tf_op jit(solution)/shard_map/psum | solution.py:77
  709.0 2.9 fusion.7
  711.8 79.8 %reduce-scatter.19.cloned.1.call-done = f32[64,128]{1,0:T(8,128)} async-done(((f32[1024,128]{1,0:T(8,128)}), f32[64,128]{1,0:T(8,128)}) %reduce-scatter.19.cloned.1.call-update) | async-done | bytes 32784
  791.6 84.0 %reduce-scatter.15.cloned.1.call-done = f32[64,128]{1,0:T(8,128)} async-done(((f32[1024,128]{1,0:T(8,128)}), f32[64,128]{1,0:T(8,128)}) %reduce-scatter.15.cloned.1.call-update) | async-done | bytes 32784 | tf_op jit(solution)/shard_map/reduce_scatter | solution.py:90
  (13 shorter events, 0.0 us)
Async XLA Ops:
  7.2 40.6 %copy-start = (bf16[1,1024,1024]{2,1,0:T(8,128)(2,1)S(1)}, bf16[1,1024,1024]{2,1,0:T(8,128)(2,1)}, u32[]{:S(2)}) copy-start(bf16[1,1024,1024]{2,1,0:T(8,128)(2,1)} %param.11) | copy-start | bytes 6291460
  7.2 40.3 %copy-start.3 = (s32[1,64]{1,0:T(1,128)S(1)}, s32[1,64]{1,0:T(1,128)}, u32[]{:S(2)}) copy-start(s32[1,64]{1,0:T(1,128)} %param.13) | copy-start | bytes 772
  7.2 229.1 %all-reduce.4.cloned.1.call-start = ((), (), s32[]{:S(2)}) async-start(), calls=%async_computation.12 | async-start | bytes 1048576
  47.8 6.5 copy-start.4
  47.8 6.6 copy-start.5
  47.8 6.6 copy-start.6
  47.8 6.6 copy-start.7
  60.2 2.0 copy-start.1
  60.2 3.7 copy-start.8
  62.1 177.5 %copy-start.2 = (bf16[1,4,1024]{2,1,0:T(4,128)(2,1)S(1)}, bf16[1,4,1024]{2,1,0:T(4,128)(2,1)}, u32[]{:S(2)}) copy-start(bf16[1,4,1024]{2,1,0:T(4,128)(2,1)} %param.10) | copy-start | bytes 24580
  63.8 282.4 %reduce-scatter.17.cloned.1.call-start = ((), (), s32[]{:S(2)}) async-start(), calls=%async_computation.9 | async-start | bytes 4456448 | tf_op jit(solution)/shard_map/reduce_scatter | solution.py:86
  242.4 247.7 %reduce-scatter.11.cloned.1.call-start = ((), (), s32[]{:S(2)}) async-start(), calls=%async_computation.6 | async-start | bytes 8912896 | tf_op jit(solution)/shard_map/reduce_scatter | solution.py:84
  251.6 382.1 %reduce-scatter.13.cloned.1.call-start = ((), (), s32[]{:S(2)}) async-start(), calls=%async_computation.7 | async-start | bytes 8912896 | tf_op jit(solution)/shard_map/reduce_scatter | solution.py:85
  258.2 453.6 %reduce-scatter.21.cloned.1.call-start = ((), (), s32[]{:S(2)}) async-start(), calls=%async_computation.11 | async-start | bytes 557056
  348.2 443.4 %reduce-scatter.19.cloned.1.call-start = ((), (), s32[]{:S(2)}) async-start(), calls=%async_computation.10 | async-start | bytes 557056
  492.2 383.3 %reduce-scatter.15.cloned.1.call-start = ((), (), s32[]{:S(2)}) async-start(), calls=%async_computation.8 | async-start | bytes 557056 | tf_op jit(solution)/shard_map/reduce_scatter | solution.py:90
Sparse Core Ops, SparseCore 0:
  63.9 172.2 all-reduce.3
  242.5 103.6 reduce-scatter.16
  350.8 139.2 reduce-scatter.10
  494.6 138.9 reduce-scatter.12
  636.5 70.4 reduce-scatter.20
  710.1 81.3 reduce-scatter.18
  794.6 80.8 reduce-scatter.14
where the time goes:
time: 893 us; the launch traced here: 882 us
  waiting for transfers between devices  706 us (79%)
  blocking collectives  110 us (12%)
  matrix products  43.3 us (5%)
  between operations  15 us (2%)
    unnamed x10, waiting for transfers between devices  251 us
    reduce_scatter x1, waiting for transfers between devices, local(): lax.psum_scatter(cand_term, 'dev', scatter_dimension=1, tiled=True)  142 us
    reduce_scatter x1, waiting for transfers between devices, local(): lax.psum_scatter(user_term, 'dev', scatter_dimension=1, tiled=True)  141 us
    reduce_scatter x1, waiting for transfers between devices, local(): lax.psum_scatter(enc_term, 'dev', scatter_dimension=1, tiled=True)  88 us
    reduce_scatter x1, waiting for transfers between devices, local(): lax.psum_scatter(user_cols_sum, 'grp', scatter_dimension=0, tiled=True)  84 us
    psum x1, blocking collectives, local(): lax.psum((scorer_term, bias_term), ('grp', 'dev'))  75.3 us
    all_gather x1, blocking collectives, local(): proj_all = lax.all_gather(user_proj, 'dev', axis=0, tiled=True)  35.1 us
    dot_general x4, matrix products, contract_first(): lax.dot_general(left, right, (((0,), (0,)), ((), ())), precision=precisio...  24.1 us
  transfers between devices with their start and end apart: 7, of which 6 were waited for; matrix products, arithmetic and copies ran while one was open for 3% of the time, Pallas kernels for 0%

commit v1 on v0

v1 whole, which is shorter than its diff:
```python
import jax
import jax.numpy as jnp
from jax import lax
from jax.experimental import pallas as pl
from jax.experimental.pallas import tpu as pltpu
from jax.sharding import PartitionSpec as P

f32 = jnp.float32
bf16 = jnp.bfloat16
MESH = pl.DeviceIdType.MESH

D = 1024
H = 2048
C = 1024
SLOTS = 64
KAUG = D + 128
ROWS = D + SLOTS
CHUNK = 256


def ds(start, size):
    return pl.ds(pl.multiple_of(start, size), size)


def split(value):
    high = value.astype(bf16).astype(f32)
    return high, value - high


def kernel(
    hist_ref,
    dscore_ref,
    counts_ref,
    slot_ref,
    bias_ref,
    scorer_ref,
    cand_hbm,
    we_hbm,
    wu_hbm,
    wc_hbm,
    cg_ref,
    ug_ref,
    eg_ref,
    sc_ref,
    bi_ref,
    hg_ref,
    xs,
    xt,
    we,
    wu,
    wcs,
    dcol,
    z,
    hp32,
    hgat,
    hgat32,
    h32,
    uh,
    eslope,
    grx,
    part,
    csend,
    crecv,
    s32,
    asend,
    arecv,
    aown,
    bsend,
    brecv,
    bown,
    ssend,
    srecv,
    sown,
    msg,
    sgf,
    mrecv,
    a2send,
    a2recv,
    b2send,
    b2recv,
    tt32,
    zsend,
    zrecv,
    ug32,
    enc,
    erecv,
    fsend,
    frecv,
    ld,
    h_s,
    h_r,
    g_s,
    g_r,
    c_s,
    c_r,
    a_s,
    a_r,
    b_s,
    b_r,
    s_s,
    s_r,
    md_s,
    md_r,
    mg_s,
    mg_r,
    a2_s,
    a2_r,
    b2_s,
    b2_r,
    z_s,
    z_r,
    e_s,
    e_r,
    f_s,
    f_r,
):
    g = lax.axis_index("grp")
    d = lax.axis_index("dev")
    y, zl = lax.div(g, 4), lax.rem(g, 4)
    zh, x, c = lax.div(d, 8), lax.rem(lax.div(d, 2), 4), lax.rem(d, 2)

    def dev_of(zh_, x_):
        return zh_ * 8 + x_ * 2 + c

    def block_of(k):
        zh_ = lax.rem(zh + 1 + lax.div(k, 4), 2)
        x_ = lax.rem(x + 1 + lax.rem(k, 4), 4)
        return zh_, x_

    def remote(src, dst, send, recv, to):
        return pltpu.make_async_remote_copy(
            src_ref=src,
            dst_ref=dst,
            send_sem=send,
            recv_sem=recv,
            device_id=to,
            device_id_type=MESH,
        )

    loads = [
        pltpu.make_async_copy(we_hbm, we, ld.at[0]),
        pltpu.make_async_copy(cand_hbm.at[0], xs.at[:, pl.ds(0, D)], ld.at[1]),
        pltpu.make_async_copy(wu_hbm, wu, ld.at[2]),
        pltpu.make_async_copy(wc_hbm, wcs.at[pl.ds(0, D)], ld.at[3]),
    ]
    for load in loads:
        load.start()

    barrier = pltpu.get_barrier_semaphore()

    @pl.loop(1, 16)
    def _(j):
        pl.semaphore_signal(
            barrier, inc=1, device_id=(g, lax.rem(d + j, 16)), device_id_type=MESH
        )
        pl.semaphore_signal(
            barrier, inc=1, device_id=(lax.rem(g + j, 16), d), device_id_type=MESH
        )

    @pl.loop(1, 4)
    def _(j):
        pl.semaphore_signal(
            barrier,
            inc=1,
            device_id=(y * 4 + lax.rem(zl + j, 4), dev_of(1 - zh, x)),
            device_id_type=MESH,
        )

    hist = hist_ref[0].astype(f32)
    for k in range(8):
        hp32[pl.ds(4 * k, 4), :] = hist[:, 128 * k : 128 * k + 128]
    hgat[d] = hp32[...].astype(bf16)
    pl.semaphore_wait(barrier, 33)

    def hist_copy(j):
        return remote(
            hgat.at[d], hgat.at[d], h_s.at[j], h_r.at[j], (g, lax.rem(d + j, 16))
        )

    @pl.loop(1, 16)
    def _(j):
        hist_copy(j).start()

    r_i = lax.broadcasted_iota(jnp.int32, (SLOTS, SLOTS), 0)
    c_i = lax.broadcasted_iota(jnp.int32, (SLOTS, SLOTS), 1)
    counts = jnp.broadcast_to(counts_ref[...], (SLOTS, SLOTS)).astype(f32)
    slots = jnp.broadcast_to(slot_ref[...], (SLOTS, SLOTS)).astype(f32)
    ends = jnp.sum(jnp.where(c_i <= r_i, counts, 0.0), axis=1, keepdims=True)
    starts = jnp.sum(jnp.where(c_i < r_i, counts, 0.0), axis=1, keepdims=True)
    mine = jnp.sum(jnp.where(c_i == r_i, slots, 0.0), axis=1, keepdims=True)
    r_w = lax.broadcasted_iota(jnp.int32, (SLOTS, 128), 1).astype(f32)
    hit = r_w == mine
    start_row = jnp.sum(jnp.where(hit, starts, 0.0), axis=0, keepdims=True)
    end_row = jnp.sum(jnp.where(hit, ends, 0.0), axis=0, keepdims=True)
    base = (d * C).astype(f32)
    lane = lax.broadcasted_iota(jnp.int32, (CHUNK, 128), 1)
    ones = jnp.where((lane >= SLOTS) & (lane < SLOTS + 3), 1.0, 0.0)
    for r in range(C // CHUNK):
        row = lax.broadcasted_iota(jnp.int32, (CHUNK, 128), 0).astype(f32) + (base + r * CHUNK)
        sel = jnp.where((row >= start_row) & (row < end_row), 1.0, 0.0)
        xs[pl.ds(r * CHUNK, CHUNK), pl.ds(D, 128)] = (sel + ones).astype(bf16)
        for q in range(CHUNK // 128):
            xt[pl.ds(D, SLOTS), pl.ds(r * CHUNK + q * 128, 128)] = (
                sel[q * 128 : q * 128 + 128].T[:SLOTS].astype(bf16)
            )
    for r in range(8):
        dcol[pl.ds(r * 128, 128), :] = jnp.broadcast_to(dscore_ref[r : r + 1, :], (128, 128)).T
    loads[1].wait()
    for r in range(4):
        for q in range(4):
            xt[pl.ds(q * 256, 256), pl.ds(r * 256, 256)] = xs[
                pl.ds(r * 256, 256), pl.ds(q * 256, 256)
            ].T

    @pl.loop(1, 16)
    def _(j):
        hist_copy(j).wait_recv()

    hgat32[...] = hgat[...].astype(f32).reshape(512, 128)
    for i in range(16):
        for k in range(8):
            h32[pl.ds(4 * i, 4), pl.ds(128 * k, 128)] = hgat32[pl.ds(32 * i + 4 * k, 4), :]
    uh[pl.ds(64, 64), :] = h32[...].astype(bf16)
    loads[0].wait()
    pre = jnp.dot(uh[pl.ds(64, 64), :], we[...], preferred_element_type=f32)
    sig = 0.5 * jnp.tanh(0.5 * pre) + 0.5
    act = pre * sig
    eslope[...] = sig + act * (1.0 - sig)
    uh[pl.ds(0, 64), :] = (h32[...] + act).astype(bf16)

    def group_copy(j):
        g_to = lax.rem(g + j, 16)
        return remote(
            uh.at[:, ds(lax.div(g_to, 2) * 128, 128)],
            grx.at[g],
            g_s.at[j],
            g_r.at[j],
            (g_to, d),
        )

    @pl.loop(1, 16)
    def _(j):
        group_copy(j).start()

    grx[g] = uh[:, ds(lax.div(g, 2) * 128, 128)]
    loads[2].wait()
    loads[3].wait()

    def core_copy(k):
        return remote(csend.at[k], crecv.at[k], c_s.at[k], c_r.at[k], (g, d + 1 - 2 * c))

    def a_copy(k):
        _, x_ = block_of(k)
        return remote(asend.at[k], arecv.at[k], a_s.at[k], a_r.at[k], (g, dev_of(zh, x_)))

    def b_copy(k, j):
        y_ = lax.rem(y + j, 4)
        return remote(
            bsend.at[k, y_], brecv.at[k, j], b_s.at[k * 4 + j], b_r.at[k * 4 + j], (y_ * 4 + zl, d)
        )

    def s_copy(k):
        return remote(ssend.at[k], srecv.at[k], s_s.at[k], s_r.at[k], (g, dev_of(*block_of(k))))

    def both(ref, n, rows=slice(None)):
        first = ref[rows, ds(n * 256 + c * 128, 128)]
        second = ref[rows, ds(n * 256 + (1 - c) * 128, 128)]
        return jnp.concatenate([first, second], axis=1)

    def compute(k):
        zh_, x_ = block_of(k)
        n = zh_ * 4 + x_
        proj = jnp.dot(uh[pl.ds(0, 64), :], both(wu, n), preferred_element_type=f32).astype(bf16)
        bias = both(bias_ref, n)
        b0, rest = split(bias)
        b1, b2 = split(rest)
        line = lax.broadcasted_iota(jnp.int32, (64, 256), 0)
        tail = jnp.where(line == 0, b0, jnp.where(line == 1, b1, jnp.where(line == 2, b2, 0.0)))
        weights = jnp.concatenate(
            [both(wcs, n, pl.ds(0, D)), proj, tail.astype(bf16)], axis=0
        )
        scorer = both(scorer_ref, n)
        total = jnp.zeros((8, 256), f32)
        for r in range(C // CHUNK):
            rows = pl.ds(r * CHUNK, CHUNK)
            v = jnp.dot(xs[rows, :], weights, preferred_element_type=f32)
            sigma = 0.5 * jnp.tanh(0.5 * v) + 0.5
            hidden = v * sigma
            slope = sigma + hidden * (1.0 - sigma)
            score = dcol[rows, :]
            score = jnp.concatenate([score, score], axis=1)
            z[rows, :] = (score * scorer * slope).astype(bf16)
            total = total + jnp.sum((score * hidden).reshape(CHUNK // 8, 8, 256), axis=0)
        term = jnp.dot(xt[...], z[...], preferred_element_type=f32)
        part[lax.rem(k, 2), pl.ds(0, ROWS), :] = term[:, :128]
        csend[k, pl.ds(0, ROWS), :] = term[:, 128:].astype(bf16)
        s_hi, s_lo = split(jnp.sum(total, axis=0, keepdims=True))
        line = lax.broadcasted_iota(jnp.int32, (16, 256), 0)
        aux = jnp.where(line == 0, s_hi, jnp.where(line == 1, s_lo, 0.0))
        part[lax.rem(k, 2), pl.ds(ROWS, 16), :] = aux[:, :128]
        csend[k, pl.ds(ROWS, 16), :] = aux[:, 128:].astype(bf16)
        core_copy(k).start()

    def stage(k):
        core_copy(k).wait_recv()
        total = part[lax.rem(k, 2)] + crecv[k].astype(f32)
        s32[...] = total
        half = total.astype(bf16)
        for y_ in range(4):
            asend[k, pl.ds(y_ * 128, 128), :] = half[y_ * 256 : y_ * 256 + 128]
            bsend[k, y_] = half[y_ * 256 + 128 : y_ * 256 + 256]

        @pl.loop(1, 4)
        def _(j):
            b_copy(k, j).start()

        @pl.when(lax.rem(k, 4) != 3)
        def _():
            a_copy(k).start()

        @pl.when(lax.rem(k, 4) == 3)
        def _():
            for y_ in range(4):
                aown[lax.div(k, 4), pl.ds(y_ * 128, 128), :] = s32[pl.ds(y_ * 256, 128), :]

        line = lax.broadcasted_iota(jnp.int32, (16, 128), 0)
        aux = total[ROWS:]
        t_hi, t_lo = split(aux[0:1] + aux[1:2])
        tail = jnp.where(line == 0, t_hi, jnp.where(line == 1, t_lo, 0.0))

        @pl.when(k != 7)
        def _():
            ssend[k, pl.ds(0, SLOTS), :] = half[D:ROWS]
            ssend[k, pl.ds(SLOTS, 16), :] = tail.astype(bf16)
            s_copy(k).start()

        @pl.when(k == 7)
        def _():
            sown[pl.ds(0, SLOTS), :] = total[D:ROWS]
            sown[pl.ds(SLOTS, 16), :] = tail

        bown[k] = s32[pl.ds(pl.multiple_of(y * 256 + 128, 128), 128), :]

    @pl.loop(0, 8)
    def _(k):
        compute(k)

        @pl.when(k > 0)
        def _():
            stage(k - 1)

    stage(7)

    slot_sum = sown[...]
    for k in range(7):
        s_copy(k).wait_recv()
        slot_sum = slot_sum + srecv[k].astype(f32)
    rows64 = slot_sum[:SLOTS]
    b_hi, b_lo = split(jnp.sum(rows64, axis=0, keepdims=True))
    q_hi, q_lo = split(slot_sum[SLOTS : SLOTS + 1] + slot_sum[SLOTS + 1 : SLOTS + 2])
    line = lax.broadcasted_iota(jnp.int32, (16, 128), 0)
    tail = jnp.where(
        line == 0,
        b_hi,
        jnp.where(line == 1, b_lo, jnp.where(line == 2, q_hi, jnp.where(line == 3, q_lo, 0.0))),
    )
    msg[pl.ds(0, SLOTS), :] = rows64.astype(bf16)
    msg[pl.ds(SLOTS, 16), :] = tail.astype(bf16)

    def dev_msg(j):
        return remote(
            msg.at[pl.ds(0, SLOTS)],
            sgf.at[:, ds(d * 128, 128)],
            md_s.at[j],
            md_r.at[j],
            (g, lax.rem(d + j, 16)),
        )

    def grp_msg(j):
        return remote(msg, mrecv.at[g], mg_s.at[j], mg_r.at[j], (lax.rem(g + j, 16), d))

    @pl.loop(1, 16)
    def _(j):
        dev_msg(j).start()

    sgf[:, ds(d * 128, 128)] = msg[pl.ds(0, SLOTS), :]
    mrecv[g] = msg[...]

    def a2_copy(j):
        y_ = lax.rem(y + j, 4)
        return remote(a2send.at[y_], a2recv.at[j], a2_s.at[j], a2_r.at[j], (y_ * 4 + zl, d))

    def b2_copy(k):
        _, x_ = block_of(k)
        return remote(b2send.at[k], b2recv.at[k], b2_s.at[k], b2_r.at[k], (g, dev_of(zh, x_)))

    for kk in range(2):
        total = aown[kk]
        for j in range(3):
            a_copy(4 * kk + j).wait_recv()
            total = total + arecv[4 * kk + j].astype(f32)
        aown[kk] = total
        half = total.astype(bf16)
        for y_ in range(4):
            a2send[y_, kk] = half[y_ * 128 : y_ * 128 + 128]

    @pl.loop(1, 4)
    def _(j):
        a2_copy(j).start()

    @pl.loop(0, 8)
    def _(k):
        total = bown[k]
        for j in range(1, 4):
            b_copy(k, j).wait_recv()
            total = total + brecv[k, j].astype(f32)
        bown[k] = total
        b2send[k] = total.astype(bf16)

        @pl.when(lax.rem(k, 4) != 3)
        def _():
            b2_copy(k).start()

    @pl.loop(1, 16)
    def _(j):
        grp_msg(j).start()

    @pl.loop(1, 16)
    def _(j):
        dev_msg(j).wait_recv()

    user_grad = lax.dot_general(
        sgf[...], wu[...], (((1,), (1,)), ((), ())), preferred_element_type=f32
    )
    ug32[...] = user_grad
    enc[...] = (user_grad * eslope[...]).astype(bf16)

    def enc_copy(j):
        return remote(
            enc.at[:, ds(lax.div(d, 2) * 128, 128)],
            erecv.at[g],
            e_s.at[j],
            e_r.at[j],
            (lax.rem(g + j, 16), d),
        )

    @pl.loop(1, 16)
    def _(j):
        enc_copy(j).start()

    erecv[g] = enc[:, ds(lax.div(d, 2) * 128, 128)]

    @pl.loop(1, 4)
    def _(j):
        a2_copy(j).wait_recv()

    for kk in range(2):
        ta = aown[kk, pl.ds(pl.multiple_of(y * 128, 128), 128), :]
        for j in range(1, 4):
            ta = ta + a2recv[j, kk].astype(f32)
        tb = bown[4 * kk + 3]
        for j in range(3):
            b2_copy(4 * kk + j).wait_recv()
            tb = tb + b2recv[4 * kk + j].astype(f32)
        for zl_, piece in enumerate((ta[:64], ta[64:], tb[:64], tb[64:])):
            tt32[kk, zl_] = piece
            zsend[kk, zl_] = piece.astype(bf16)

    def z_copy(kk, j):
        zl_ = lax.rem(zl + j, 4)
        zh_ = lax.rem(zh + 1 + kk, 2)
        return remote(
            zsend.at[kk, zl_],
            zrecv.at[kk, j],
            z_s.at[kk * 4 + j],
            z_r.at[kk * 4 + j],
            (y * 4 + zl_, dev_of(zh_, x)),
        )

    for kk, j in [(0, 0), (0, 1), (0, 2), (0, 3), (1, 1), (1, 2), (1, 3)]:
        z_copy(kk, j).start()

    eight = ds(lax.div(d, 2) * 8, 8)
    ug_rows = ug32[eight, :]
    enc_rows = (ug_rows * eslope[eight, :]).astype(bf16)
    hist_grad = ug_rows + lax.dot_general(
        enc_rows, we[...], (((1,), (1,)), ((), ())), preferred_element_type=f32
    )
    hg_ref[0] = jnp.where(c == 0, hist_grad[:4], hist_grad[4:])

    @pl.loop(1, 16)
    def _(j):
        group_copy(j).wait_recv()
        grp_msg(j).wait_recv()

    user_cols = grx[:, pl.ds(0, 64), :].reshape(1024, 128)
    hist_cols = grx[:, pl.ds(64, 64), :].reshape(1024, 128)
    slot_cols = mrecv[:, pl.ds(0, 64), :].reshape(1024, 128)
    user_out = jnp.dot(user_cols.T, slot_cols, preferred_element_type=f32)
    odd = lax.rem(g, 2)
    ug_ref[...] = jnp.where(odd == 0, user_out[:64], user_out[64:])
    tails = jnp.sum(mrecv[:, pl.ds(64, 16), :].astype(f32), axis=0)
    line = lax.broadcasted_iota(jnp.int32, (8, 128), 0)
    fsend[...] = jnp.where(
        line == 0, tails[0:1] + tails[1:2], jnp.where(line == 1, tails[2:3] + tails[3:4], 0.0)
    )

    def f_copy(j):
        return remote(fsend, frecv.at[d], f_s.at[j], f_r.at[j], (g, lax.rem(d + j, 16)))

    @pl.loop(1, 16)
    def _(j):
        f_copy(j).start()

    frecv[d] = fsend[...]

    @pl.loop(1, 16)
    def _(j):
        enc_copy(j).wait_recv()

    enc_out = jnp.dot(hist_cols.T, erecv[...].reshape(1024, 128), preferred_element_type=f32)
    enc_out = jnp.where(odd == 0, enc_out[:64], enc_out[64:])
    eg_ref[...] = jnp.where(c == 0, enc_out[:, :64], enc_out[:, 64:])

    cand = tt32[1, zl]
    for kk, j in [(0, 0), (0, 1), (0, 2), (0, 3), (1, 1), (1, 2), (1, 3)]:
        z_copy(kk, j).wait_recv()
        cand = cand + zrecv[kk, j].astype(f32)
    cg_ref[...] = cand

    @pl.loop(1, 16)
    def _(j):
        f_copy(j).wait_recv()

    final = frecv[...]
    bi_ref[...] = final[:, 0, :]
    sc_ref[...] = final[:, 1, :]

    @pl.loop(1, 16)
    def _(j):
        hist_copy(j).wait_send()
        group_copy(j).wait_send()
        dev_msg(j).wait_send()
        grp_msg(j).wait_send()
        enc_copy(j).wait_send()
        f_copy(j).wait_send()

    @pl.loop(0, 8)
    def _(k):
        core_copy(k).wait_send()
        for j in range(1, 4):
            b_copy(k, j).wait_send()

        @pl.when(lax.rem(k, 4) != 3)
        def _():
            a_copy(k).wait_send()
            b2_copy(k).wait_send()

        @pl.when(k != 7)
        def _():
            s_copy(k).wait_send()

    @pl.loop(1, 4)
    def _(j):
        a2_copy(j).wait_send()

    for kk, j in [(0, 0), (0, 1), (0, 2), (0, 3), (1, 1), (1, 2), (1, 3)]:
        z_copy(kk, j).wait_send()


def local(
    history,
    candidates,
    score_grad,
    req_counts,
    owner_slot,
    encoder_weight,
    user_weight,
    cand_weight,
    hidden_bias,
    scorer_weight,
):
    vmem = pl.BlockSpec(memory_space=pltpu.VMEM)
    hbm = pl.BlockSpec(memory_space=pl.ANY)
    V = pltpu.VMEM
    dma = lambda n: pltpu.SemaphoreType.DMA((n,))
    scratch = [
        V((C, KAUG), bf16),
        V((ROWS, C), bf16),
        V((D, D), bf16),
        V((D, H), bf16),
        V((D, H), bf16),
        V((C, 128), f32),
        V((C, 256), bf16),
        V((32, 128), f32),
        V((16, 32, 128), bf16),
        V((512, 128), f32),
        V((64, D), f32),
        V((128, D), bf16),
        V((64, D), f32),
        V((16, 128, 128), bf16),
        V((2, ROWS + 16, 128), f32),
        V((8, ROWS + 16, 128), bf16),
        V((8, ROWS + 16, 128), bf16),
        V((ROWS + 16, 128), f32),
        V((8, 512, 128), bf16),
        V((8, 512, 128), bf16),
        V((2, 512, 128), f32),
        V((8, 4, 128, 128), bf16),
        V((8, 4, 128, 128), bf16),
        V((8, 128, 128), f32),
        V((8, 80, 128), bf16),
        V((8, 80, 128), bf16),
        V((80, 128), f32),
        V((80, 128), bf16),
        V((64, H), bf16),
        V((16, 80, 128), bf16),
        V((4, 2, 128, 128), bf16),
        V((4, 2, 128, 128), bf16),
        V((8, 128, 128), bf16),
        V((8, 128, 128), bf16),
        V((2, 4, 64, 128), f32),
        V((2, 4, 64, 128), bf16),
        V((2, 4, 64, 128), bf16),
        V((64, D), f32),
        V((64, D), bf16),
        V((16, 64, 128), bf16),
        V((8, 128), f32),
        V((16, 8, 128), f32),
        dma(4),
    ]
    for n in (16, 16, 8, 8, 32, 8, 16, 16, 4, 8, 8, 16, 16):
        scratch += [dma(n), dma(n)]
    outs = pl.pallas_call(
        kernel,
        out_shape=(
            jax.ShapeDtypeStruct((64, 128), f32),
            jax.ShapeDtypeStruct((64, 128), f32),
            jax.ShapeDtypeStruct((64, 64), f32),
            jax.ShapeDtypeStruct((16, 128), f32),
            jax.ShapeDtypeStruct((16, 128), f32),
            jax.ShapeDtypeStruct((1, 4, D), f32),
        ),
        in_specs=[vmem] * 6 + [hbm] * 4,
        out_specs=(vmem,) * 6,
        scratch_shapes=scratch,
        compiler_params=pltpu.CompilerParams(
            collective_id=0, has_side_effects=True, vmem_limit_bytes=56 * 2**20
        ),
        name="ranking_backward",
    )(
        history,
        score_grad.reshape(8, 128),
        req_counts,
        owner_slot,
        hidden_bias.reshape(1, H),
        scorer_weight.reshape(1, H),
        candidates,
        encoder_weight,
        user_weight,
        cand_weight,
    )
    cg, ug, eg, sc, bi, hg = outs
    return (cg, ug, eg, sc.reshape(H), bi.reshape(H), hg)


def solution(mesh):
    in_specs = (
        P("grp", "dev", None),
        P("grp", "dev", None),
        P("grp", "dev"),
        P("grp", None),
        P("grp", None),
        P(),
        P(),
        P(),
        P(),
        P(),
    )
    out_specs = (P("grp", "dev"), P("grp", "dev"), P("grp", "dev"), P(), P(), P("grp", "dev", None))
    return jax.shard_map(local, mesh=mesh, in_specs=in_specs, out_specs=out_specs, check_vma=False)
```

time: 893 us -> 79.7 us (0.09); the launches traced: 882 us -> 79.3 us
  waiting for transfers between devices: 706 us -> 0 us
  blocking collectives: 110 us -> 0 us
  Pallas kernels: 0 us -> 70.6 us
  matrix products: 43.3 us -> 0 us
  between operations: 15 us -> 0.65 us
    reduce_scatter x4 -> x0, waiting for transfers between devices: 455 us -> none  [the longest x1 142 us: local(): lax.psum_scatter(cand_term, 'dev', scatter_dimension=1, tiled=True)]
    unnamed x10 -> x0, waiting for transfers between devices: 251 us -> none
    psum x1 -> x0, blocking collectives: 75.3 us -> none  [local(): lax.psum((scorer_term, bias_term), ('grp', 'dev'))]
    pallas_call x0 -> x1, Pallas kernels: none -> 70.6 us  [local(): pl.pallas_call(kernel, out_shape=(jax.ShapeDtypeStruct((64, 128), f32), j...]
    dot_general x10 -> x0, matrix products: 43.3 us -> none  [the longest x4 24.1 us: contract_first(): lax.dot_general(left, right, (((0,), (0,)), ((), ())), precision=precisio...]
    all_gather x1 -> x0, blocking collectives: 35.1 us -> none  [local(): proj_all = lax.all_gather(user_proj, 'dev', axis=0, tiled=True)]
  transfers between devices with their start and end apart: 7 -> 0, of which waited for: 6 -> 0; matrix products, arithmetic and copies ran while one was open for 3% -> 0% of each run, Pallas kernels for 0% -> 0%
where the time goes in v1:
time: 79.7 us; the launch traced here: 79.3 us
  Pallas kernels  70.6 us (89%)
  local copies, waits for them, and re-layouts  8.03 us (10%)
    pallas_call x1, Pallas kernels, local(): pl.pallas_call(kernel, out_shape=(jax.ShapeDtypeStruct((64, 128), f32), j...  70.6 us
    unnamed x6, local copies, waits for them, and re-layouts  8.03 us

profile of v1, /device:TPU:1, one launch (start us, length us, event | category | flops | bytes accessed | tf_op | source)
XLA Modules:
  0.0 79.3 jit_solution(11667750640725509801)
XLA Ops:
  0.6 70.6 %ranking_backward.1 = (f32[64,128]{1,0:T(8,128)}, f32[64,128]{1,0:T(8,128)}, f32[64,64]{1,0:T(8,128)}, f32[16,128]{1,0:T(8,128)}, f32[16,128]{1,0:T(8,128)}, /*index=5*/f32[1,4,1024]{2,1,0:T(4,128)}) custom-call(bf16[1,4,1024]{2,1,0:T(4,128)(2,1)} %hist_ref.1, f32[8,128]{1,0:T(8,128)} %bitcast.9, s32[1,64]{1,0:T(1,128)} %counts_ref.1, s32[1,64]{1,0:T(1,128)} %slot_ref.1, ...), custom_call_target="tpu_custom_call" | custom-call | tf_op jit(solution)/shard_map/ranking_backward/pallas_call | solution.py:634
  71.2 1.4 %copy.22 = f32[64,128]{1,0:T(8,128)} copy(f32[64,128]{1,0:T(8,128)} %get-tuple-element.24) | data formatting | bytes 65536
  72.6 1.4 %copy.23 = f32[64,128]{1,0:T(8,128)} copy(f32[64,128]{1,0:T(8,128)} %get-tuple-element.25) | data formatting | bytes 65536
  74.0 1.4 %copy.24 = f32[64,64]{1,0:T(8,128)} copy(f32[64,64]{1,0:T(8,128)} %get-tuple-element.26) | data formatting | bytes 32768
  75.3 1.3 %copy.25 = f32[2048]{0:T(1024)} copy(f32[2048]{0:T(1024)} %bitcast.6) | data formatting | bytes 16384
  76.6 1.3 %copy.26 = f32[2048]{0:T(1024)} copy(f32[2048]{0:T(1024)} %bitcast.5) | data formatting | bytes 16384
  77.9 1.3 %copy.27 = f32[1,4,1024]{2,1,0:T(4,128)} copy(f32[1,4,1024]{2,1,0:T(4,128)} %get-tuple-element.29) | data formatting | bytes 32768

commit v2 on v1

v2 whole, which is shorter than its diff:
```python
import jax
import jax.numpy as jnp
from jax import lax
from jax.experimental import pallas as pl
from jax.experimental.pallas import tpu as pltpu
from jax.sharding import PartitionSpec as P

f32 = jnp.float32
bf16 = jnp.bfloat16
MESH = pl.DeviceIdType.MESH

D = 1024
H = 2048
C = 1024
SLOTS = 64
ROWS = D + SLOTS
HALF = 512
PACKED = 288
CHUNK = 256


def ds(start, size):
    return pl.ds(pl.multiple_of(start, size), size)


def split(value):
    high = value.astype(bf16).astype(f32)
    return high, value - high


def kernel(
    hist_ref,
    dscore_ref,
    counts_ref,
    slot_ref,
    bias_ref,
    scorer_ref,
    cand_hbm,
    we_hbm,
    wu_hbm,
    wc_hbm,
    out_ref,
    xs,
    sel_s,
    xt,
    we,
    wu,
    wc,
    dcol,
    ahead,
    z0,
    z1,
    picked0,
    picked1,
    acts,
    hp32,
    hgat,
    hgat32,
    h32,
    uh,
    eslope,
    grx,
    part,
    csend,
    crecv,
    s32,
    lsend,
    lrecv,
    lown,
    asend,
    arecv,
    aown,
    bsend,
    brecv,
    bown,
    ssend,
    srecv,
    msg,
    sgf,
    mrecv,
    a2send,
    a2recv,
    b2send,
    b2recv,
    tt32,
    zsend,
    zrecv,
    ug32,
    enc,
    erecv,
    u32,
    usend,
    urecv,
    n32,
    nsend,
    nrecv,
    tsend,
    trecv,
    frecv,
    ld,
    h_s,
    h_r,
    g_s,
    g_r,
    c_s,
    c_r,
    a_s,
    a_r,
    b_s,
    b_r,
    l_s,
    l_r,
    s_s,
    s_r,
    md_s,
    md_r,
    my_s,
    my_r,
    a2_s,
    a2_r,
    b2_s,
    b2_r,
    z_s,
    z_r,
    e_s,
    e_r,
    u_s,
    u_r,
    n_s,
    n_r,
    t_s,
    t_r,
    f_s,
    f_r,
):
    g = lax.axis_index("grp")
    d = lax.axis_index("dev")
    y, zl = lax.div(g, 4), lax.rem(g, 4)
    zh, x, c = lax.div(d, 8), lax.rem(lax.div(d, 2), 4), lax.rem(d, 2)
    chip = lax.div(d, 2)
    other = d + 1 - 2 * c
    far = lax.rem(d + 8, 16)

    def dev_of(zh_, x_):
        return zh_ * 8 + x_ * 2 + c

    def chip_peer(j):
        return (g, lax.rem(chip + j, 8) * 2 + c)

    def y_peer(j):
        return (lax.rem(y + j, 4) * 4 + zl, d)

    def z_peer(kk, j):
        return (y * 4 + lax.rem(zl + j, 4), dev_of(lax.rem(zh + 1 + kk, 2), x))

    def block_of(k):
        zh_ = lax.rem(zh + 1 + lax.div(k, 4), 2)
        i = lax.rem(k, 4)
        x_ = lax.rem(x + 2 + 3 * i + 3 * lax.div(i * (i - 1), 2), 4)
        return zh_, x_

    def remote(src, dst, send, recv, to):
        return pltpu.make_async_remote_copy(
            src_ref=src,
            dst_ref=dst,
            send_sem=send,
            recv_sem=recv,
            device_id=to,
            device_id_type=MESH,
        )

    def gather(ref_of, send, recv):
        def own(j):
            return remote(ref_of(d), ref_of(d), send.at[j], recv.at[j], chip_peer(j))

        def beside():
            return remote(ref_of(d), ref_of(d), send.at[0], recv.at[0], (g, other))

        def onward(j):
            i = lax.rem(chip + 8 - j, 8) * 2 + c
            return remote(ref_of(i), ref_of(i), send.at[8 + j], recv.at[8 + j], (g, other))

        def start():
            @pl.loop(1, 8)
            def _(j):
                own(j).start()

            beside().start()

        def forward_all():
            @pl.loop(1, 8)
            def _(j):
                own(j).wait_recv()
                onward(j).start()

        def finish_recv():
            beside().wait_recv()

            @pl.loop(1, 8)
            def _(j):
                onward(j).wait_recv()

        def finish_send():
            beside().wait_send()

            @pl.loop(1, 8)
            def _(j):
                own(j).wait_send()
                onward(j).wait_send()

        return start, forward_all, finish_recv, finish_send

    loads = [
        pltpu.make_async_copy(cand_hbm.at[0], xs, ld.at[0]),
        pltpu.make_async_copy(wc_hbm, wc, ld.at[1]),
        pltpu.make_async_copy(we_hbm, we, ld.at[2]),
        pltpu.make_async_copy(wu_hbm, wu, ld.at[3]),
    ]
    for load in loads:
        load.start()

    barrier = pltpu.get_barrier_semaphore()

    def greet(to):
        pl.semaphore_signal(barrier, inc=1, device_id=to, device_id_type=MESH)

    greet((g, other))

    @pl.loop(1, 4)
    def _(j):
        greet(z_peer(0, j))
        greet(z_peer(1, j))
        greet(y_peer(j))

    @pl.loop(1, 8)
    def _(j):
        greet(chip_peer(j))

    hist = hist_ref[0].astype(f32)
    for k in range(8):
        hp32[pl.ds(4 * k, 4), :] = hist[:, 128 * k : 128 * k + 128]
    hgat[d] = hp32[...].astype(bf16)
    hist_start, hist_forward, hist_recv, hist_send = gather(lambda i: hgat.at[i], h_s, h_r)

    def both(ref, n, rows=slice(None)):
        first = ref[rows, ds(n * 256 + c * 128, 128)]
        second = ref[rows, ds(n * 256 + (1 - c) * 128, 128)]
        return jnp.concatenate([first, second], axis=1)

    def number(k):
        zh_, x_ = block_of(k)
        return zh_ * 4 + x_

    def forward(k):
        ahead[k] = jnp.dot(xs[...], both(wc, number(k)), preferred_element_type=f32)

    pl.semaphore_wait(barrier, 17)
    hist_start()

    r_i = lax.broadcasted_iota(jnp.int32, (SLOTS, SLOTS), 0)
    c_i = lax.broadcasted_iota(jnp.int32, (SLOTS, SLOTS), 1)
    counts = jnp.broadcast_to(counts_ref[...], (SLOTS, SLOTS)).astype(f32)
    slots = jnp.broadcast_to(slot_ref[...], (SLOTS, SLOTS)).astype(f32)
    ends = jnp.sum(jnp.where(c_i <= r_i, counts, 0.0), axis=1, keepdims=True)
    starts = jnp.sum(jnp.where(c_i < r_i, counts, 0.0), axis=1, keepdims=True)
    mine = jnp.sum(jnp.where(c_i == r_i, slots, 0.0), axis=1, keepdims=True)
    r_w = lax.broadcasted_iota(jnp.int32, (SLOTS, 128), 1).astype(f32)
    hit = r_w == mine
    start_row = jnp.sum(jnp.where(hit, starts, 0.0), axis=0, keepdims=True)
    end_row = jnp.sum(jnp.where(hit, ends, 0.0), axis=0, keepdims=True)
    base = (d * C).astype(f32)
    lane = lax.broadcasted_iota(jnp.int32, (CHUNK, 128), 1)
    ones = jnp.where((lane >= SLOTS) & (lane < SLOTS + 3), 1.0, 0.0)
    for r in range(C // CHUNK):
        row = lax.broadcasted_iota(jnp.int32, (CHUNK, 128), 0).astype(f32) + (base + r * CHUNK)
        sel = jnp.where((row >= start_row) & (row < end_row), 1.0, 0.0)
        sel_s[pl.ds(r * CHUNK, CHUNK), :] = (sel + ones).astype(bf16)
        for q in range(CHUNK // 128):
            xt[pl.ds(D, SLOTS), pl.ds(r * CHUNK + q * 128, 128)] = (
                sel[q * 128 : q * 128 + 128].T[:SLOTS].astype(bf16)
            )
    for r in range(8):
        dcol[pl.ds(r * 128, 128), :] = jnp.broadcast_to(dscore_ref[r : r + 1, :], (128, 128)).T

    loads[0].wait()
    loads[1].wait()

    @pl.loop(0, 4)
    def _(k):
        forward(k)

    hist_forward()

    for r in range(4):
        for q in range(4):
            xt[pl.ds(q * 256, 256), pl.ds(r * 256, 256)] = xs[
                pl.ds(r * 256, 256), pl.ds(q * 256, 256)
            ].T

    @pl.loop(4, 8)
    def _(k):
        forward(k)

    hist_recv()

    hgat32[...] = hgat[...].astype(f32).reshape(512, 128)
    for i in range(16):
        for k in range(8):
            h32[pl.ds(4 * i, 4), pl.ds(128 * k, 128)] = hgat32[pl.ds(32 * i + 4 * k, 4), :]
    uh[pl.ds(64, 64), :] = h32[...].astype(bf16)
    loads[2].wait()
    pre = jnp.dot(uh[pl.ds(64, 64), :], we[...], preferred_element_type=f32)
    sig = 0.5 * jnp.tanh(0.5 * pre) + 0.5
    act = pre * sig
    eslope[...] = sig + act * (1.0 - sig)
    uh[pl.ds(0, 64), :] = (h32[...] + act).astype(bf16)

    def group_copy(j):
        y_ = lax.rem(y + j, 4)
        return remote(uh.at[:, ds(y_ * 256, 256)], grx.at[y], g_s.at[j], g_r.at[j], y_peer(j))

    @pl.loop(1, 4)
    def _(j):
        group_copy(j).start()

    grx[y] = uh[:, ds(y * 256, 256)]
    loads[3].wait()

    def core_copy(k):
        return remote(csend.at[k], crecv.at[k], c_s.at[k], c_r.at[k], (g, other))

    def a_copy(k):
        _, x_ = block_of(k)
        return remote(asend.at[k], arecv.at[k], a_s.at[k], a_r.at[k], (g, dev_of(zh, x_)))

    def b_copy(k, j):
        y_ = lax.rem(y + j, 4)
        return remote(bsend.at[k, y_], brecv.at[k, j], b_s.at[k * 4 + j], b_r.at[k * 4 + j], y_peer(j))

    def line_copy(k):
        _, x_ = block_of(k)
        return remote(lsend.at[k], lrecv.at[k], l_s.at[k], l_r.at[k], (g, dev_of(zh, x_)))

    def s_copy():
        return remote(ssend, srecv, s_s.at[0], s_r.at[0], (g, far))

    def a2_copy(kk, j):
        y_ = lax.rem(y + j, 4)
        i = kk * 4 + j
        return remote(a2send.at[kk, y_], a2recv.at[kk, j], a2_s.at[i], a2_r.at[i], y_peer(j))

    def b2_copy(k):
        _, x_ = block_of(k)
        return remote(b2send.at[k], b2recv.at[k], b2_s.at[k], b2_r.at[k], (g, dev_of(zh, x_)))

    def stack(rows, first):
        line = lax.broadcasted_iota(jnp.int32, (16, rows[0].shape[1]), 0)
        out = jnp.zeros((16, rows[0].shape[1]), f32)
        for i, value in enumerate(rows):
            out = jnp.where(line == first + i, value, out)
        return out

    def project(k, picked):
        n = number(k)
        proj = jnp.dot(uh[pl.ds(0, 64), :], both(wu, n), preferred_element_type=f32)
        b0, rest = split(both(bias_ref, n))
        b1, b2 = split(rest)
        picked[pl.ds(0, 64), :] = proj.astype(bf16)
        picked[pl.ds(64, 16), :] = stack([b0, b1, b2], 0).astype(bf16)

    def step(k, z_to, picked, z_from=None, picked_to=None):
        scorer = both(scorer_ref, number(k))
        total = jnp.zeros((8, 256), f32)
        for r in range(C // HALF):
            rows = pl.ds(r * HALF, HALF)
            v = ahead[k, rows, :] + jnp.dot(
                sel_s[rows, :], picked[...], preferred_element_type=f32
            )
            sigma = 0.5 * jnp.tanh(0.5 * v) + 0.5
            hidden = v * sigma
            slope = sigma + hidden * (1.0 - sigma)
            score = dcol[rows, :]
            score = jnp.concatenate([score, score], axis=1)
            z_to[rows, :] = (score * scorer * slope).astype(bf16)
            total = total + jnp.sum((score * hidden).reshape(HALF // 8, 8, 256), axis=0)
            if z_from is not None:
                product(k - 1, r, z_from)
        acts[k] = total
        if picked_to is not None:
            project(k + 1, picked_to)
        if z_from is not None:
            finish(k - 1)

    def product(k, r, z_from):
        rows = pl.ds(r * (ROWS // 2), ROWS // 2)
        term = jnp.dot(xt[rows, :], z_from[...], preferred_element_type=f32)
        part[lax.rem(k, 2), rows, :] = term[:, :128]
        csend[k, rows, :] = term[:, 128:].astype(bf16)

    def finish(k):
        aux = stack(split(jnp.sum(acts[k], axis=0, keepdims=True)), 0)
        part[lax.rem(k, 2), pl.ds(ROWS, 16), :] = aux[:, :128]
        csend[k, pl.ds(ROWS, 16), :] = aux[:, 128:].astype(bf16)
        core_copy(k).start()

    def stage(k):
        core_copy(k).wait_recv()
        total = part[lax.rem(k, 2)] + crecv[k].astype(f32)
        s32[...] = total
        half = total.astype(bf16)
        aux = total[ROWS:]
        tail = stack(split(aux[0:1] + aux[1:2]), 0)

        @pl.when(lax.rem(k, 4) != 3)
        def _():
            lsend[k, pl.ds(0, SLOTS), :] = half[D:ROWS]
            lsend[k, pl.ds(SLOTS, 16), :] = tail.astype(bf16)
            line_copy(k).start()

        for y_ in range(4):
            asend[k, pl.ds(y_ * 128, 128), :] = half[y_ * 256 : y_ * 256 + 128]
            bsend[k, y_] = half[y_ * 256 + 128 : y_ * 256 + 256]

        @pl.loop(1, 4)
        def _(j):
            b_copy(k, j).start()

        @pl.when(lax.rem(k, 4) != 3)
        def _():
            a_copy(k).start()

        @pl.when(lax.rem(k, 4) == 3)
        def _():
            for y_ in range(4):
                aown[lax.div(k, 4), pl.ds(y_ * 128, 128), :] = s32[pl.ds(y_ * 256, 128), :]
            lown[lax.div(k, 4), pl.ds(0, SLOTS), :] = s32[pl.ds(D, SLOTS), :]
            lown[lax.div(k, 4), pl.ds(SLOTS, 16), :] = tail

        bown[k] = s32[pl.ds(pl.multiple_of(y * 256 + 128, 128), 128), :]

    def slot_line(kk):
        total = lown[kk]
        for j in range(3):
            line_copy(4 * kk + j).wait_recv()
            total = total + lrecv[4 * kk + j].astype(f32)
        return total

    def a_second(kk):
        total = aown[kk]
        for j in range(3):
            a_copy(4 * kk + j).wait_recv()
            total = total + arecv[4 * kk + j].astype(f32)
        aown[kk] = total
        half = total.astype(bf16)
        for y_ in range(4):
            a2send[kk, y_] = half[y_ * 128 : y_ * 128 + 128]

        @pl.loop(1, 4)
        def _(j):
            a2_copy(kk, j).start()

    def b_second(k):
        total = bown[k]
        for j in range(1, 4):
            b_copy(k, j).wait_recv()
            total = total + brecv[k, j].astype(f32)
        bown[k] = total
        b2send[k] = total.astype(bf16)

        @pl.when(lax.rem(k, 4) != 3)
        def _():
            b2_copy(k).start()

    for picked in (picked0, picked1):
        picked[pl.ds(64, 64), :] = jnp.zeros((64, 256), bf16)
    project(0, picked0)
    step(0, z0, picked0, None, picked1)

    @pl.loop(0, 3)
    def _(i):
        k = 2 * i
        step(k + 1, z1, picked1, z0, picked0)

        @pl.when(i > 0)
        def _():
            stage(k - 1)

        step(k + 2, z0, picked0, z1, picked1)
        stage(k)

        @pl.when(i == 2)
        def _():
            total = slot_line(0)
            ssend[pl.ds(0, SLOTS), :] = total[:SLOTS].astype(bf16)
            ssend[pl.ds(SLOTS, 16), :] = stack(
                split(total[SLOTS : SLOTS + 1] + total[SLOTS + 1 : SLOTS + 2]), 0
            ).astype(bf16)
            s_copy().start()

    step(7, z1, picked1, z0)
    stage(5)
    for r in range(2):
        product(7, r, z1)
    finish(7)
    stage(6)

    @pl.loop(1, 4)
    def _(j):
        group_copy(j).wait_recv()

    user_cols = grx[:, pl.ds(0, 64), :].reshape(256, 256).T
    hist_cols = grx[:, pl.ds(64, 64), :].reshape(256, 256).T
    stage(7)

    s_copy().wait_recv()
    slot_sum = slot_line(1) + srecv[...].astype(f32)
    rows64 = slot_sum[:SLOTS]
    tail = stack(
        split(jnp.sum(rows64, axis=0, keepdims=True))
        + split(slot_sum[SLOTS : SLOTS + 1] + slot_sum[SLOTS + 1 : SLOTS + 2]),
        0,
    )
    msg[pl.ds(0, SLOTS), :] = rows64.astype(bf16)
    msg[pl.ds(SLOTS, 16), :] = tail.astype(bf16)
    sgf[:, ds(d * 128, 128)] = rows64.astype(bf16)
    slot_start, slot_forward, slot_recv, slot_send = gather(
        lambda i: sgf.at[:, ds(i * 128, 128)], md_s, md_r
    )

    def y_msg(j):
        return remote(msg, mrecv.at[y], my_s.at[j], my_r.at[j], y_peer(j))

    slot_start()

    mrecv[y] = msg[...]

    @pl.loop(1, 4)
    def _(j):
        y_msg(j).start()

    def u_copy(j):
        zl_ = lax.rem(zl + j, 4)
        return remote(usend.at[zl_], urecv.at[j], u_s.at[j], u_r.at[j], z_peer(1, j))

    def t_copy(j):
        return remote(tsend, trecv.at[j], t_s.at[j], t_r.at[j], z_peer(1, j))

    @pl.loop(0, 4)
    def _(k):
        b_second(k)

    a_second(0)
    @pl.loop(1, 4)
    def _(j):
        y_msg(j).wait_recv()

    tails = jnp.sum(mrecv[:, pl.ds(64, 16), :].astype(f32), axis=0)
    tsend[...] = stack([tails[0:1] + tails[1:2], tails[2:3] + tails[3:4]], 0)[:8]

    @pl.loop(1, 4)
    def _(j):
        t_copy(j).start()

    user_part = jnp.dot(
        user_cols, mrecv[:, pl.ds(0, 64), :].reshape(256, 128), preferred_element_type=f32
    ).reshape(4, 64, 128)
    u32[...] = user_part
    usend[...] = user_part.astype(bf16)

    @pl.loop(1, 4)
    def _(j):
        u_copy(j).start()

    @pl.loop(4, 8)
    def _(k):
        b_second(k)

    a_second(1)

    slot_forward()
    slot_recv()
    totals = tsend[...]
    for j in range(1, 4):
        t_copy(j).wait_recv()
        totals = totals + trecv[j]
    frecv[d] = totals
    f_start, f_forward, f_recv, f_send = gather(lambda i: frecv.at[i], f_s, f_r)
    f_start()


    user_grad = lax.dot_general(
        sgf[...], wu[...], (((1,), (1,)), ((), ())), preferred_element_type=f32
    )
    ug32[...] = user_grad
    enc[...] = (user_grad * eslope[...]).astype(bf16)
    own_cols = ds(lax.div(d, 2) * 128, 128)

    def enc_copy(j):
        return remote(enc.at[:, own_cols], erecv.at[y], e_s.at[j], e_r.at[j], y_peer(j))

    @pl.loop(1, 4)
    def _(j):
        enc_copy(j).start()

    erecv[y] = enc[:, own_cols]

    for kk in range(2):
        ta = aown[kk, pl.ds(pl.multiple_of(y * 128, 128), 128), :]
        tb = bown[4 * kk + 3]
        for j in range(1, 4):
            a2_copy(kk, j).wait_recv()
            ta = ta + a2recv[kk, j].astype(f32)
            b2_copy(4 * kk + j - 1).wait_recv()
            tb = tb + b2recv[4 * kk + j - 1].astype(f32)
        for zl_, piece in enumerate((ta[:64], ta[64:], tb[:64], tb[64:])):
            tt32[kk, zl_] = piece
            zsend[kk, zl_] = piece.astype(bf16)

    def z_copy(kk, j):
        zl_ = lax.rem(zl + j, 4)
        i = kk * 4 + j
        return remote(zsend.at[kk, zl_], zrecv.at[kk, j], z_s.at[i], z_r.at[i], z_peer(kk, j))

    z_all = [(0, 0), (0, 1), (0, 2), (0, 3), (1, 1), (1, 2), (1, 3)]
    for kk, j in z_all:
        z_copy(kk, j).start()

    @pl.loop(1, 4)
    def _(j):
        enc_copy(j).wait_recv()

    enc_part = jnp.dot(hist_cols, erecv[...].reshape(256, 128), preferred_element_type=f32)
    enc_part = jnp.where(c == 0, enc_part[:, :64], enc_part[:, 64:]).reshape(4, 2, 32, 64)
    enc_part = jnp.concatenate([enc_part[:, 0], enc_part[:, 1]], axis=2)
    n32[...] = enc_part
    nsend[...] = enc_part.astype(bf16)

    def n_copy(j):
        zl_ = lax.rem(zl + j, 4)
        return remote(nsend.at[zl_], nrecv.at[j], n_s.at[j], n_r.at[j], z_peer(1, j))

    @pl.loop(1, 4)
    def _(j):
        n_copy(j).start()

    f_forward()

    eight = ds(lax.div(d, 2) * 8, 8)
    ug_rows = ug32[eight, :]
    enc_rows = (ug_rows * eslope[eight, :]).astype(bf16)
    hist_grad = ug_rows + lax.dot_general(
        enc_rows, we[...], (((1,), (1,)), ((), ())), preferred_element_type=f32
    )
    hist_grad = jnp.where(c == 0, hist_grad[:4], hist_grad[4:])
    for k in range(8):
        out_ref[pl.ds(224 + 8 * k, 4), :] = hist_grad[:, 128 * k : 128 * k + 128]

    user_out = u32[zl]
    for j in range(1, 4):
        u_copy(j).wait_recv()
        user_out = user_out + urecv[j].astype(f32)
    out_ref[pl.ds(64, 64), :] = user_out

    cand = tt32[1, zl]
    for kk, j in z_all:
        z_copy(kk, j).wait_recv()
        cand = cand + zrecv[kk, j].astype(f32)
    out_ref[pl.ds(0, 64), :] = cand

    enc_out = n32[zl]
    for j in range(1, 4):
        n_copy(j).wait_recv()
        enc_out = enc_out + nrecv[j].astype(f32)
    out_ref[pl.ds(128, 32), pl.ds(0, 64)] = enc_out[:, :64]
    out_ref[pl.ds(160, 32), pl.ds(0, 64)] = enc_out[:, 64:]

    f_recv()

    final = frecv[...]
    out_ref[pl.ds(192, 16), :] = final[:, 1, :]
    out_ref[pl.ds(208, 16), :] = final[:, 0, :]

    hist_send()
    slot_send()
    f_send()
    s_copy().wait_send()

    @pl.loop(0, 8)
    def _(k):
        core_copy(k).wait_send()
        for j in range(1, 4):
            b_copy(k, j).wait_send()

        @pl.when(lax.rem(k, 4) != 3)
        def _():
            a_copy(k).wait_send()
            b2_copy(k).wait_send()
            line_copy(k).wait_send()

    @pl.loop(1, 4)
    def _(j):
        group_copy(j).wait_send()
        y_msg(j).wait_send()
        enc_copy(j).wait_send()
        u_copy(j).wait_send()
        t_copy(j).wait_send()
        n_copy(j).wait_send()
        for kk in range(2):
            a2_copy(kk, j).wait_send()

    for kk, j in z_all:
        z_copy(kk, j).wait_send()


def unpack(packed, cg_ref, ug_ref, eg_ref, sc_ref, bi_ref, hg_ref):
    cg_ref[...] = packed[pl.ds(0, 64), :]
    ug_ref[...] = packed[pl.ds(64, 64), :]
    eg_ref[...] = packed[pl.ds(128, 64), pl.ds(0, 64)]
    sc_ref[...] = packed[pl.ds(192, 16), :]
    bi_ref[...] = packed[pl.ds(208, 16), :]
    for k in range(8):
        hg_ref[0, :, pl.ds(128 * k, 128)] = packed[pl.ds(224 + 8 * k, 4), :]


def local(
    history,
    candidates,
    score_grad,
    req_counts,
    owner_slot,
    encoder_weight,
    user_weight,
    cand_weight,
    hidden_bias,
    scorer_weight,
):
    vmem = pl.BlockSpec(memory_space=pltpu.VMEM)
    hbm = pl.BlockSpec(memory_space=pl.ANY)
    V = pltpu.VMEM
    dma = lambda n: pltpu.SemaphoreType.DMA((n,))
    scratch = [
        V((C, D), bf16),
        V((C, 128), bf16),
        V((ROWS, C), bf16),
        V((D, D), bf16),
        V((D, H), bf16),
        V((D, H), bf16),
        V((C, 128), f32),
        V((8, C, 256), f32),
        V((C, 256), bf16),
        V((C, 256), bf16),
        V((128, 256), bf16),
        V((128, 256), bf16),
        V((8, 8, 256), f32),
        V((32, 128), f32),
        V((16, 32, 128), bf16),
        V((512, 128), f32),
        V((64, D), f32),
        V((128, D), bf16),
        V((64, D), f32),
        V((4, 128, 256), bf16),
        V((2, ROWS + 16, 128), f32),
        V((8, ROWS + 16, 128), bf16),
        V((8, ROWS + 16, 128), bf16),
        V((ROWS + 16, 128), f32),
        V((8, 80, 128), bf16),
        V((8, 80, 128), bf16),
        V((2, 80, 128), f32),
        V((8, 512, 128), bf16),
        V((8, 512, 128), bf16),
        V((2, 512, 128), f32),
        V((8, 4, 128, 128), bf16),
        V((8, 4, 128, 128), bf16),
        V((8, 128, 128), f32),
        V((80, 128), bf16),
        V((80, 128), bf16),
        V((80, 128), bf16),
        V((64, H), bf16),
        V((4, 80, 128), bf16),
        V((2, 4, 128, 128), bf16),
        V((2, 4, 128, 128), bf16),
        V((8, 128, 128), bf16),
        V((8, 128, 128), bf16),
        V((2, 4, 64, 128), f32),
        V((2, 4, 64, 128), bf16),
        V((2, 4, 64, 128), bf16),
        V((64, D), f32),
        V((64, D), bf16),
        V((4, 64, 128), bf16),
        V((4, 64, 128), f32),
        V((4, 64, 128), bf16),
        V((4, 64, 128), bf16),
        V((4, 32, 128), f32),
        V((4, 32, 128), bf16),
        V((4, 32, 128), bf16),
        V((8, 128), f32),
        V((4, 8, 128), f32),
        V((16, 8, 128), f32),
        dma(4),
    ]
    for n in (16, 4, 8, 8, 32, 8, 1, 16, 4, 8, 8, 8, 4, 4, 4, 4, 16):
        scratch += [dma(n), dma(n)]
    packed = pl.pallas_call(
        kernel,
        out_shape=jax.ShapeDtypeStruct((PACKED, 128), f32),
        in_specs=[vmem] * 6 + [hbm] * 4,
        out_specs=vmem,
        scratch_shapes=scratch,
        compiler_params=pltpu.CompilerParams(
            collective_id=0, has_side_effects=True, vmem_limit_bytes=56 * 2**20
        ),
        name="ranking_backward",
    )(
        history,
        score_grad.reshape(8, 128),
        req_counts,
        owner_slot,
        hidden_bias.reshape(1, H),
        scorer_weight.reshape(1, H),
        candidates,
        encoder_weight,
        user_weight,
        cand_weight,
    )
    cg, ug, eg, sc, bi, hg = pl.pallas_call(
        unpack,
        out_shape=(
            jax.ShapeDtypeStruct((64, 128), f32),
            jax.ShapeDtypeStruct((64, 128), f32),
            jax.ShapeDtypeStruct((64, 64), f32),
            jax.ShapeDtypeStruct((16, 128), f32),
            jax.ShapeDtypeStruct((16, 128), f32),
            jax.ShapeDtypeStruct((1, 4, D), f32),
        ),
        in_specs=[vmem],
        out_specs=(vmem,) * 6,
        name="unpack",
    )(packed)
    return (cg, ug, eg, sc.reshape(H), bi.reshape(H), hg)


def solution(mesh):
    in_specs = (
        P("grp", "dev", None),
        P("grp", "dev", None),
        P("grp", "dev"),
        P("grp", None),
        P("grp", None),
        P(),
        P(),
        P(),
        P(),
        P(),
    )
    out_specs = (P("grp", "dev"), P("grp", "dev"), P("grp", "dev"), P(), P(), P("grp", "dev", None))
    return jax.shard_map(local, mesh=mesh, in_specs=in_specs, out_specs=out_specs, check_vma=False)
```

time: 79.7 us -> 61.9 us (0.78)
  Pallas kernels: 70.6 us -> 61.1 us
  local copies, waits for them, and re-layouts: 8.03 us -> 0 us
    pallas_call x1 -> x2, Pallas kernels: 70.6 us -> 61.1 us  [the longest x1 59.6 us: local(): pl.pallas_call(kernel, out_shape=jax.ShapeDtypeStruct((PACKED, 128), f32)...]
    unnamed x6 -> x0, local copies, waits for them, and re-layouts: 8.03 us -> none
where the time goes in v2:
time: 61.9 us; the launch traced here: 61.8 us
  Pallas kernels  61.1 us (99%)
  between operations  0.64 us (1%)
    pallas_call x1, Pallas kernels, local(): pl.pallas_call(kernel, out_shape=jax.ShapeDtypeStruct((PACKED, 128), f32)...  59.6 us
    pallas_call x1, Pallas kernels, local(): pl.pallas_call(unpack, out_shape=(jax.ShapeDtypeStruct((64, 128), f32), j...  1.56 us

profile of v2, /device:TPU:1, one launch (start us, length us, event | category | flops | bytes accessed | tf_op | source)
XLA Modules:
  0.0 61.8 jit_solution(2028571606757762591)
XLA Ops:
  0.6 59.6 %ranking_backward.1.packed = f32[288,128]{1,0:T(8,128)} custom-call(bf16[1,4,1024]{2,1,0:T(4,128)(2,1)} %hist_ref.1, f32[8,128]{1,0:T(8,128)} %bitcast.7, s32[1,64]{1,0:T(1,128)} %counts_ref.1, s32[1,64]{1,0:T(1,128)} %slot_ref.1, f32[1,2048]{1,0:T(1,128)} %bitcast.5, f32[1,2048]{1,0:T(1,128)} %bitcast.6, bf16[1,1024,1024]{2,1,0:T(8,128)(2,1)} %cand_hbm.1, ...), custom_call_target="tpu_custom_call" | custom-call | tf_op jit(solution)/shard_map/ranking_backward/pallas_call | solution.py:803
  60.2 1.6 %unpack.1 = (f32[64,128]{1,0:T(8,128)}, f32[64,128]{1,0:T(8,128)}, f32[64,64]{1,0:T(8,128)}, f32[16,128]{1,0:T(8,128)}, f32[16,128]{1,0:T(8,128)}, /*index=5*/f32[1,4,1024]{2,1,0:T(4,128)}) custom-call(f32[288,128]{1,0:T(8,128)} %ranking_backward.1.packed), custom_call_target="tpu_custom_call" | custom-call | tf_op jit(solution)/shard_map/unpack/pallas_call | solution.py:825

commit v3 on v2

--- a/solution.py
+++ b/solution.py
@@ -29,20 +29,27 @@
 
 
 def kernel(
+    hist_hbm,
+    dscore_hbm,
+    counts_hbm,
+    slot_hbm,
+    bias_hbm,
+    scorer_hbm,
+    cand_hbm,
+    we_hbm,
+    wu_hbm,
+    wc_hbm,
+    out_ref,
     hist_ref,
     dscore_ref,
     counts_ref,
     slot_ref,
     bias_ref,
     scorer_ref,
-    cand_hbm,
-    we_hbm,
-    wu_hbm,
-    wc_hbm,
-    out_ref,
     xs,
     sel_s,
     xt,
+    selt,
     we,
     wu,
     wc,
@@ -50,9 +57,8 @@
     ahead,
     z0,
     z1,
-    picked0,
-    picked1,
-    acts,
+    z2,
+    picked,
     hp32,
     hgat,
     hgat32,
@@ -64,9 +70,8 @@
     csend,
     crecv,
     s32,
-    lsend,
-    lrecv,
-    lown,
+    ahalf,
+    bhalf,
     asend,
     arecv,
     aown,
@@ -75,6 +80,7 @@
     bown,
     ssend,
     srecv,
+    sown,
     msg,
     sgf,
     mrecv,
@@ -85,7 +91,6 @@
     tt32,
     zsend,
     zrecv,
-    ug32,
     enc,
     erecv,
     u32,
@@ -102,14 +107,18 @@
     h_r,
     g_s,
     g_r,
+    go_s,
+    go_r,
+    ah_s,
+    ah_r,
+    bh_s,
+    bh_r,
     c_s,
     c_r,
     a_s,
     a_r,
     b_s,
     b_r,
-    l_s,
-    l_r,
     s_s,
     s_r,
     md_s,
@@ -139,7 +148,6 @@
     zh, x, c = lax.div(d, 8), lax.rem(lax.div(d, 2), 4), lax.rem(d, 2)
     chip = lax.div(d, 2)
     other = d + 1 - 2 * c
-    far = lax.rem(d + 8, 16)
 
     def dev_of(zh_, x_):
         return zh_ * 8 + x_ * 2 + c
@@ -216,7 +224,20 @@
         pltpu.make_async_copy(we_hbm, we, ld.at[2]),
         pltpu.make_async_copy(wu_hbm, wu, ld.at[3]),
     ]
-    for load in loads:
+    small = [
+        pltpu.make_async_copy(src, dst, ld.at[4 + i])
+        for i, (src, dst) in enumerate(
+            (
+                (hist_hbm, hist_ref),
+                (dscore_hbm, dscore_ref),
+                (counts_hbm, counts_ref),
+                (slot_hbm, slot_ref),
+                (bias_hbm, bias_ref),
+                (scorer_hbm, scorer_ref),
+            )
+        )
+    ]
+    for load in small + loads:
         load.start()
 
     barrier = pltpu.get_barrier_semaphore()
@@ -224,7 +245,9 @@
     def greet(to):
         pl.semaphore_signal(barrier, inc=1, device_id=to, device_id_type=MESH)
 
-    greet((g, other))
+    @pl.loop(1, 16)
+    def _(j):
+        greet((g, lax.rem(d + j, 16)))
 
     @pl.loop(1, 4)
     def _(j):
@@ -232,9 +255,8 @@
         greet(z_peer(1, j))
         greet(y_peer(j))
 
-    @pl.loop(1, 8)
-    def _(j):
-        greet(chip_peer(j))
+    for load in small:
+        load.wait()
 
     hist = hist_ref[0].astype(f32)
     for k in range(8):
@@ -254,7 +276,7 @@
     def forward(k):
         ahead[k] = jnp.dot(xs[...], both(wc, number(k)), preferred_element_type=f32)
 
-    pl.semaphore_wait(barrier, 17)
+    pl.semaphore_wait(barrier, 24)
     hist_start()
 
     r_i = lax.broadcasted_iota(jnp.int32, (SLOTS, SLOTS), 0)
@@ -276,7 +298,7 @@
         sel = jnp.where((row >= start_row) & (row < end_row), 1.0, 0.0)
         sel_s[pl.ds(r * CHUNK, CHUNK), :] = (sel + ones).astype(bf16)
         for q in range(CHUNK // 128):
-            xt[pl.ds(D, SLOTS), pl.ds(r * CHUNK + q * 128, 128)] = (
+            selt[:, pl.ds(r * CHUNK + q * 128, 128)] = (
                 sel[q * 128 : q * 128 + 128].T[:SLOTS].astype(bf16)
             )
     for r in range(8):
@@ -285,7 +307,7 @@
     loads[0].wait()
     loads[1].wait()
 
-    @pl.loop(0, 4)
+    @pl.loop(0, 7)
     def _(k):
         forward(k)
 
@@ -297,9 +319,7 @@
                 pl.ds(r * 256, 256), pl.ds(q * 256, 256)
             ].T
 
-    @pl.loop(4, 8)
-    def _(k):
-        forward(k)
+    forward(7)
 
     hist_recv()
 
@@ -315,9 +335,17 @@
     eslope[...] = sig + act * (1.0 - sig)
     uh[pl.ds(0, 64), :] = (h32[...] + act).astype(bf16)
 
+    share = pl.ds(pl.multiple_of(c * 64, 64), 64)
+
     def group_copy(j):
-        y_ = lax.rem(y + j, 4)
-        return remote(uh.at[:, ds(y_ * 256, 256)], grx.at[y], g_s.at[j], g_r.at[j], y_peer(j))
+        cols = ds(lax.rem(y + j, 4) * 256, 256)
+        return remote(
+            uh.at[share, cols], grx.at[y, share], g_s.at[j], g_r.at[j], y_peer(j)
+        )
+
+    def group_on(j):
+        part_of = grx.at[lax.rem(y + 4 - j, 4), share]
+        return remote(part_of, part_of, go_s.at[j], go_r.at[j], (g, other))
 
     @pl.loop(1, 4)
     def _(j):
@@ -333,16 +361,34 @@
         _, x_ = block_of(k)
         return remote(asend.at[k], arecv.at[k], a_s.at[k], a_r.at[k], (g, dev_of(zh, x_)))
 
+    def a_half(i):
+        x_ = lax.rem(x + 1 + 2 * i, 4)
+        return remote(
+            asend.at[0, pl.ds(256 * i, 256)],
+            ahalf.at[i],
+            ah_s.at[i],
+            ah_r.at[i],
+            (g, dev_of(zh, x_)),
+        )
+
+    def b_half(k, i):
+        y_ = lax.rem(y + 2, 4)
+        return remote(
+            bsend.at[k, y_, pl.ds(64 * i, 64)],
+            bhalf.at[k, i],
+            bh_s.at[2 * k + i],
+            bh_r.at[2 * k + i],
+            y_peer(1 + 2 * i),
+        )
+
     def b_copy(k, j):
         y_ = lax.rem(y + j, 4)
         return remote(bsend.at[k, y_], brecv.at[k, j], b_s.at[k * 4 + j], b_r.at[k * 4 + j], y_peer(j))
 
-    def line_copy(k):
-        _, x_ = block_of(k)
-        return remote(lsend.at[k], lrecv.at[k], l_s.at[k], l_r.at[k], (g, dev_of(zh, x_)))
-
-    def s_copy():
-        return remote(ssend, srecv, s_s.at[0], s_r.at[0], (g, far))
+    def s_copy(k, i):
+        zh_, x_ = block_of(k)
+        to = zh_ * 8 + x_ * 2 + (c if i == 0 else 1 - c)
+        return remote(ssend.at[k, i], srecv.at[k, i], s_s.at[2 * k + i], s_r.at[2 * k + i], (g, to))
 
     def a2_copy(kk, j):
         y_ = lax.rem(y + j, 4)
@@ -360,17 +406,21 @@
             out = jnp.where(line == first + i, value, out)
         return out
 
-    def project(k, picked):
+    def project(k):
         n = number(k)
         proj = jnp.dot(uh[pl.ds(0, 64), :], both(wu, n), preferred_element_type=f32)
         b0, rest = split(both(bias_ref, n))
         b1, b2 = split(rest)
-        picked[pl.ds(0, 64), :] = proj.astype(bf16)
-        picked[pl.ds(64, 16), :] = stack([b0, b1, b2], 0).astype(bf16)
-
-    def step(k, z_to, picked, z_from=None, picked_to=None):
+        return proj.astype(bf16), stack([b0, b1, b2], 0).astype(bf16)
+
+    def keep(made):
+        picked[pl.ds(0, 64), :] = made[0]
+        picked[pl.ds(64, 16), :] = made[1]
+
+    def step(k, z_to, i, z_from=None, first=0):
         scorer = both(scorer_ref, number(k))
         total = jnp.zeros((8, 256), f32)
+        made = project(k + 1)
         for r in range(C // HALF):
             rows = pl.ds(r * HALF, HALF)
             v = ahead[k, rows, :] + jnp.dot(
@@ -381,73 +431,85 @@
             slope = sigma + hidden * (1.0 - sigma)
             score = dcol[rows, :]
             score = jnp.concatenate([score, score], axis=1)
-            z_to[rows, :] = (score * scorer * slope).astype(bf16)
+            z_to[i, rows, :] = (score * scorer * slope).astype(bf16)
             total = total + jnp.sum((score * hidden).reshape(HALF // 8, 8, 256), axis=0)
             if z_from is not None:
-                product(k - 1, r, z_from)
-        acts[k] = total
-        if picked_to is not None:
-            project(k + 1, picked_to)
+                product(first + i, r, z_from, i)
+        keep(made)
+        sums = jnp.dot(selt[...], z_to[i], preferred_element_type=f32)
+        aux = stack(split(jnp.sum(total, axis=0, keepdims=True)), 0)
+        sown[pl.ds(0, SLOTS), :] = sums[:, :128]
+        sown[pl.ds(SLOTS, 16), :] = aux[:, :128]
+        for q in range(2):
+            ssend[k, q, pl.ds(0, SLOTS), :] = sums[:, 128 * q : 128 * q + 128].astype(bf16)
+            ssend[k, q, pl.ds(SLOTS, 16), :] = aux[:, 128 * q : 128 * q + 128].astype(bf16)
+
+        @pl.when(k != 7)
+        def _():
+            s_copy(k, 0).start()
+
+        s_copy(k, 1).start()
         if z_from is not None:
-            finish(k - 1)
-
-    def product(k, r, z_from):
-        rows = pl.ds(r * (ROWS // 2), ROWS // 2)
-        term = jnp.dot(xt[rows, :], z_from[...], preferred_element_type=f32)
+            core_copy(first + i).start()
+
+    def product(k, r, z_from, i):
+        rows = pl.ds(r * HALF, HALF)
+        term = jnp.dot(xt[rows, :], z_from[i], preferred_element_type=f32)
         part[lax.rem(k, 2), rows, :] = term[:, :128]
         csend[k, rows, :] = term[:, 128:].astype(bf16)
 
-    def finish(k):
-        aux = stack(split(jnp.sum(acts[k], axis=0, keepdims=True)), 0)
-        part[lax.rem(k, 2), pl.ds(ROWS, 16), :] = aux[:, :128]
-        csend[k, pl.ds(ROWS, 16), :] = aux[:, 128:].astype(bf16)
+    def back(k, z_from, i):
+        for r in range(C // HALF):
+            product(k, r, z_from, i)
         core_copy(k).start()
 
-    def stage(k):
+    def stage(k, direct=False):
         core_copy(k).wait_recv()
+        now = lax.rem(k, 4)
+        kk = lax.div(k, 4)
         total = part[lax.rem(k, 2)] + crecv[k].astype(f32)
-        s32[...] = total
+        s32[now] = total
         half = total.astype(bf16)
-        aux = total[ROWS:]
-        tail = stack(split(aux[0:1] + aux[1:2]), 0)
-
-        @pl.when(lax.rem(k, 4) != 3)
-        def _():
-            lsend[k, pl.ds(0, SLOTS), :] = half[D:ROWS]
-            lsend[k, pl.ds(SLOTS, 16), :] = tail.astype(bf16)
-            line_copy(k).start()
-
         for y_ in range(4):
             asend[k, pl.ds(y_ * 128, 128), :] = half[y_ * 256 : y_ * 256 + 128]
             bsend[k, y_] = half[y_ * 256 + 128 : y_ * 256 + 256]
-
-        @pl.loop(1, 4)
-        def _(j):
-            b_copy(k, j).start()
-
-        @pl.when(lax.rem(k, 4) != 3)
-        def _():
-            a_copy(k).start()
-
-        @pl.when(lax.rem(k, 4) == 3)
-        def _():
-            for y_ in range(4):
-                aown[lax.div(k, 4), pl.ds(y_ * 128, 128), :] = s32[pl.ds(y_ * 256, 128), :]
-            lown[lax.div(k, 4), pl.ds(0, SLOTS), :] = s32[pl.ds(D, SLOTS), :]
-            lown[lax.div(k, 4), pl.ds(SLOTS, 16), :] = tail
-
-        bown[k] = s32[pl.ds(pl.multiple_of(y * 256 + 128, 128), 128), :]
-
-    def slot_line(kk):
-        total = lown[kk]
-        for j in range(3):
-            line_copy(4 * kk + j).wait_recv()
-            total = total + lrecv[4 * kk + j].astype(f32)
-        return total
-
-    def a_second(kk):
+        if direct:
+            for j in range(1, 4):
+                b_copy(k, j).start()
+        else:
+            for i in range(2):
+                b_half(k, i).start()
+
+        bown[k] = s32[now, pl.ds(pl.multiple_of(y * 256 + 128, 128), 128), :]
+
+    def a_keep(kk):
+        for y_ in range(4):
+            aown[kk, pl.ds(y_ * 128, 128), :] = s32[3, pl.ds(y_ * 256, 128), :]
+
+    def middle(k):
+        now = lax.rem(k, 4)
+        for i in range(2):
+            y_ = lax.rem(y + 1 + 2 * i, 4)
+            start = pl.multiple_of(y_ * 256 + 128 + 64 * i, 64)
+            b_half(k, i).wait_recv()
+            bsend[k, y_, pl.ds(64 * i, 64), :] = (
+                s32[now, pl.ds(start, 64), :] + bhalf[k, i].astype(f32)
+            ).astype(bf16)
+            b_copy(k, 1 + 2 * i).start()
+
+    def a_middle(i):
+        a_half(i).wait_recv()
+        for y_ in range(2):
+            rows = pl.ds(256 * i + 128 * y_, 128)
+            more = ahalf[i, pl.ds(128 * y_, 128), :].astype(f32)
+            asend[1 + i, rows, :] = (
+                s32[1 + i, pl.ds(512 * i + 256 * y_, 128), :] + more
+            ).astype(bf16)
+        a_copy(1 + i).start()
+
+    def a_second(kk, came):
         total = aown[kk]
-        for j in range(3):
+        for j in came:
             a_copy(4 * kk + j).wait_recv()
             total = total + arecv[4 * kk + j].astype(f32)
         aown[kk] = total
@@ -459,9 +521,9 @@
         def _(j):
             a2_copy(kk, j).start()
 
-    def b_second(k):
+    def b_second(k, came=(1, 3)):
         total = bown[k]
-        for j in range(1, 4):
+        for j in came:
             b_copy(k, j).wait_recv()
             total = total + brecv[k, j].astype(f32)
         bown[k] = total
@@ -471,49 +533,52 @@
         def _():
             b2_copy(k).start()
 
-    for picked in (picked0, picked1):
-        picked[pl.ds(64, 64), :] = jnp.zeros((64, 256), bf16)
-    project(0, picked0)
-    step(0, z0, picked0, None, picked1)
+    picked[pl.ds(64, 64), :] = jnp.zeros((64, 256), bf16)
+    keep(project(0))
 
     @pl.loop(0, 3)
     def _(i):
-        k = 2 * i
-        step(k + 1, z1, picked1, z0, picked0)
+        step(i, z0, i)
+
+    @pl.loop(0, 3)
+    def _(i):
+        step(i + 3, z1, i, z0)
 
         @pl.when(i > 0)
         def _():
-            stage(k - 1)
-
-        step(k + 2, z0, picked0, z1, picked1)
-        stage(k)
-
-        @pl.when(i == 2)
+            stage(i - 1)
+
+        @pl.when(i == 0)
         def _():
-            total = slot_line(0)
-            ssend[pl.ds(0, SLOTS), :] = total[:SLOTS].astype(bf16)
-            ssend[pl.ds(SLOTS, 16), :] = stack(
-                split(total[SLOTS : SLOTS + 1] + total[SLOTS + 1 : SLOTS + 2]), 0
-            ).astype(bf16)
-            s_copy().start()
-
-    step(7, z1, picked1, z0)
-    stage(5)
-    for r in range(2):
-        product(7, r, z1)
-    finish(7)
-    stage(6)
-
-    @pl.loop(1, 4)
-    def _(j):
-        group_copy(j).wait_recv()
-
-    user_cols = grx[:, pl.ds(0, 64), :].reshape(256, 256).T
-    hist_cols = grx[:, pl.ds(64, 64), :].reshape(256, 256).T
-    stage(7)
-
-    s_copy().wait_recv()
-    slot_sum = slot_line(1) + srecv[...].astype(f32)
+            @pl.loop(1, 4)
+            def _(j):
+                group_copy(j).wait_recv()
+                group_on(j).start()
+
+        @pl.when(i == 1)
+        def _():
+            for q in range(2):
+                a_half(q).start()
+
+    @pl.loop(0, 2)
+    def _(i):
+        step(i + 6, z2, i, z1, 3)
+        stage(i + 2)
+        middle(i)
+
+    a_keep(0)
+    a_middle(0)
+    a_middle(1)
+    back(5, z1, 2)
+    stage(4)
+    middle(2)
+
+    slot_sum = sown[...]
+    for k in range(8):
+        for i in range(2):
+            if (k, i) != (7, 0):
+                s_copy(k, i).wait_recv()
+                slot_sum = slot_sum + srecv[k, i].astype(f32)
     rows64 = slot_sum[:SLOTS]
     tail = stack(
         split(jnp.sum(rows64, axis=0, keepdims=True))
@@ -538,6 +603,25 @@
     def _(j):
         y_msg(j).start()
 
+    a_copy(4).start()
+    back(6, z2, 0)
+    stage(5, True)
+    a_copy(5).start()
+    middle(3)
+    back(7, z2, 1)
+    stage(6, True)
+    a_copy(6).start()
+    middle(4)
+    stage(7, True)
+    a_keep(1)
+
+    @pl.loop(1, 4)
+    def _(j):
+        group_on(j).wait_recv()
+
+    user_cols = grx[:, pl.ds(0, 64), :].reshape(256, 256).T
+    hist_cols = grx[:, pl.ds(64, 64), :].reshape(256, 256).T
+
     def u_copy(j):
         zl_ = lax.rem(zl + j, 4)
         return remote(usend.at[zl_], urecv.at[j], u_s.at[j], u_r.at[j], z_peer(1, j))
@@ -545,11 +629,12 @@
     def t_copy(j):
         return remote(tsend, trecv.at[j], t_s.at[j], t_r.at[j], z_peer(1, j))
 
-    @pl.loop(0, 4)
-    def _(k):
+    for k in range(3):
         b_second(k)
-
-    a_second(0)
+    slot_forward()
+    a_second(0, (1, 2))
+    b_second(3)
+
     @pl.loop(1, 4)
     def _(j):
         y_msg(j).wait_recv()
@@ -561,50 +646,14 @@
     def _(j):
         t_copy(j).start()
 
-    user_part = jnp.dot(
-        user_cols, mrecv[:, pl.ds(0, 64), :].reshape(256, 128), preferred_element_type=f32
-    ).reshape(4, 64, 128)
-    u32[...] = user_part
-    usend[...] = user_part.astype(bf16)
-
-    @pl.loop(1, 4)
-    def _(j):
-        u_copy(j).start()
-
-    @pl.loop(4, 8)
-    def _(k):
-        b_second(k)
-
-    a_second(1)
-
-    slot_forward()
-    slot_recv()
-    totals = tsend[...]
-    for j in range(1, 4):
-        t_copy(j).wait_recv()
-        totals = totals + trecv[j]
-    frecv[d] = totals
-    f_start, f_forward, f_recv, f_send = gather(lambda i: frecv.at[i], f_s, f_r)
-    f_start()
-
-
-    user_grad = lax.dot_general(
-        sgf[...], wu[...], (((1,), (1,)), ((), ())), preferred_element_type=f32
-    )
-    ug32[...] = user_grad
-    enc[...] = (user_grad * eslope[...]).astype(bf16)
-    own_cols = ds(lax.div(d, 2) * 128, 128)
-
-    def enc_copy(j):
-        return remote(enc.at[:, own_cols], erecv.at[y], e_s.at[j], e_r.at[j], y_peer(j))
-
-    @pl.loop(1, 4)
-    def _(j):
-        enc_copy(j).start()
-
-    erecv[y] = enc[:, own_cols]
-
-    for kk in range(2):
+    def z_copy(kk, j):
+        zl_ = lax.rem(zl + j, 4)
+        i = kk * 4 + j
+        return remote(zsend.at[kk, zl_], zrecv.at[kk, j], z_s.at[i], z_r.at[i], z_peer(kk, j))
+
+    z_all = [(0, 0), (0, 1), (0, 2), (0, 3), (1, 1), (1, 2), (1, 3)]
+
+    def last_stage(kk):
         ta = aown[kk, pl.ds(pl.multiple_of(y * 128, 128), 128), :]
         tb = bown[4 * kk + 3]
         for j in range(1, 4):
@@ -615,15 +664,49 @@
         for zl_, piece in enumerate((ta[:64], ta[64:], tb[:64], tb[64:])):
             tt32[kk, zl_] = piece
             zsend[kk, zl_] = piece.astype(bf16)
-
-    def z_copy(kk, j):
-        zl_ = lax.rem(zl + j, 4)
-        i = kk * 4 + j
-        return remote(zsend.at[kk, zl_], zrecv.at[kk, j], z_s.at[i], z_r.at[i], z_peer(kk, j))
-
-    z_all = [(0, 0), (0, 1), (0, 2), (0, 3), (1, 1), (1, 2), (1, 3)]
-    for kk, j in z_all:
-        z_copy(kk, j).start()
+        for j in range(kk, 4):
+            z_copy(kk, j).start()
+
+    slot_recv()
+    own_cols = ds(chip * 128, 128)
+    grad_cols = lax.dot_general(
+        sgf[...], wu[own_cols, :], (((1,), (1,)), ((), ())), preferred_element_type=f32
+    )
+    enc[...] = (grad_cols * eslope[:, own_cols]).astype(bf16)
+
+    def enc_copy(j):
+        return remote(enc, erecv.at[y], e_s.at[j], e_r.at[j], y_peer(j))
+
+    @pl.loop(1, 4)
+    def _(j):
+        enc_copy(j).start()
+
+    erecv[y] = enc[...]
+
+    user_part = jnp.dot(
+        user_cols, mrecv[:, pl.ds(0, 64), :].reshape(256, 128), preferred_element_type=f32
+    ).reshape(4, 64, 128)
+    u32[...] = user_part
+    usend[...] = user_part.astype(bf16)
+
+    @pl.loop(1, 4)
+    def _(j):
+        u_copy(j).start()
+
+    totals = tsend[...]
+    for j in range(1, 4):
+        t_copy(j).wait_recv()
+        totals = totals + trecv[j]
+    frecv[d] = totals
+    f_start, f_forward, f_recv, f_send = gather(lambda i: frecv.at[i], f_s, f_r)
+    f_start()
+
+    b_second(4)
+    for k in (5, 6, 7):
+        b_second(k, (1, 2, 3))
+    a_second(1, (0, 1, 2))
+
+    last_stage(0)
 
     @pl.loop(1, 4)
     def _(j):
@@ -643,17 +726,24 @@
     def _(j):
         n_copy(j).start()
 
-    f_forward()
-
-    eight = ds(lax.div(d, 2) * 8, 8)
-    ug_rows = ug32[eight, :]
-    enc_rows = (ug_rows * eslope[eight, :]).astype(bf16)
-    hist_grad = ug_rows + lax.dot_general(
+    last_stage(1)
+
+    sixteen = ds(lax.div(d, 4) * 16, 16)
+    grad_rows = lax.dot_general(
+        sgf[sixteen, :], wu[...], (((1,), (1,)), ((), ())), preferred_element_type=f32
+    )
+    enc_rows = (grad_rows * eslope[sixteen, :]).astype(bf16)
+    hist_all = grad_rows + lax.dot_general(
         enc_rows, we[...], (((1,), (1,)), ((), ())), preferred_element_type=f32
     )
-    hist_grad = jnp.where(c == 0, hist_grad[:4], hist_grad[4:])
+    place = lax.rem(d, 4)
+    hist_grad = hist_all[:4]
+    for i in range(1, 4):
+        hist_grad = jnp.where(place == i, hist_all[4 * i : 4 * i + 4], hist_grad)
     for k in range(8):
         out_ref[pl.ds(224 + 8 * k, 4), :] = hist_grad[:, 128 * k : 128 * k + 128]
+
+    f_forward()
 
     user_out = u32[zl]
     for j in range(1, 4):
@@ -683,23 +773,40 @@
     hist_send()
     slot_send()
     f_send()
-    s_copy().wait_send()
 
     @pl.loop(0, 8)
     def _(k):
         core_copy(k).wait_send()
-        for j in range(1, 4):
-            b_copy(k, j).wait_send()
+        s_copy(k, 1).wait_send()
+
+        @pl.when(k != 7)
+        def _():
+            s_copy(k, 0).wait_send()
+
+        b_copy(k, 1).wait_send()
+        b_copy(k, 3).wait_send()
+
+        @pl.when(k < 5)
+        def _():
+            for i in range(2):
+                b_half(k, i).wait_send()
+
+        @pl.when(k >= 5)
+        def _():
+            b_copy(k, 2).wait_send()
 
         @pl.when(lax.rem(k, 4) != 3)
         def _():
+            b2_copy(k).wait_send()
+
+        @pl.when((lax.rem(k, 4) != 3) & (k > 0))
+        def _():
             a_copy(k).wait_send()
-            b2_copy(k).wait_send()
-            line_copy(k).wait_send()
 
     @pl.loop(1, 4)
     def _(j):
         group_copy(j).wait_send()
+        group_on(j).wait_send()
         y_msg(j).wait_send()
         enc_copy(j).wait_send()
         u_copy(j).wait_send()
@@ -707,6 +814,9 @@
         n_copy(j).wait_send()
         for kk in range(2):
             a2_copy(kk, j).wait_send()
+
+    for i in range(2):
+        a_half(i).wait_send()
 
     for kk, j in z_all:
         z_copy(kk, j).wait_send()
@@ -739,19 +849,25 @@
     V = pltpu.VMEM
     dma = lambda n: pltpu.SemaphoreType.DMA((n,))
     scratch = [
+        V((1, 4, D), bf16),
+        V((8, 128), f32),
+        V((1, SLOTS), jnp.int32),
+        V((1, SLOTS), jnp.int32),
+        V((1, H), f32),
+        V((1, H), f32),
         V((C, D), bf16),
         V((C, 128), bf16),
-        V((ROWS, C), bf16),
+        V((D, C), bf16),
+        V((SLOTS, C), bf16),
         V((D, D), bf16),
         V((D, H), bf16),
         V((D, H), bf16),
         V((C, 128), f32),
         V((8, C, 256), f32),
-        V((C, 256), bf16),
-        V((C, 256), bf16),
+        V((3, C, 256), bf16),
+        V((3, C, 256), bf16),
+        V((2, C, 256), bf16),
         V((128, 256), bf16),
-        V((128, 256), bf16),
-        V((8, 8, 256), f32),
         V((32, 128), f32),
         V((16, 32, 128), bf16),
         V((512, 128), f32),
@@ -759,21 +875,21 @@
         V((128, D), bf16),
         V((64, D), f32),
         V((4, 128, 256), bf16),
-        V((2, ROWS + 16, 128), f32),
-        V((8, ROWS + 16, 128), bf16),
-        V((8, ROWS + 16, 128), bf16),
-        V((ROWS + 16, 128), f32),
-        V((8, 80, 128), bf16),
-        V((8, 80, 128), bf16),
-        V((2, 80, 128), f32),
+        V((2, D, 128), f32),
+        V((8, D, 128), bf16),
+        V((8, D, 128), bf16),
+        V((4, D, 128), f32),
+        V((2, 256, 128), bf16),
+        V((5, 2, 64, 128), bf16),
         V((8, 512, 128), bf16),
         V((8, 512, 128), bf16),
         V((2, 512, 128), f32),
         V((8, 4, 128, 128), bf16),
         V((8, 4, 128, 128), bf16),
         V((8, 128, 128), f32),
-        V((80, 128), bf16),
-        V((80, 128), bf16),
+        V((8, 2, 80, 128), bf16),
+        V((8, 2, 80, 128), bf16),
+        V((80, 128), f32),
         V((80, 128), bf16),
         V((64, H), bf16),
         V((4, 80, 128), bf16),
@@ -784,8 +900,7 @@
         V((2, 4, 64, 128), f32),
         V((2, 4, 64, 128), bf16),
         V((2, 4, 64, 128), bf16),
-        V((64, D), f32),
-        V((64, D), bf16),
+        V((64, 128), bf16),
         V((4, 64, 128), bf16),
         V((4, 64, 128), f32),
         V((4, 64, 128), bf16),
@@ -796,14 +911,14 @@
         V((8, 128), f32),
         V((4, 8, 128), f32),
         V((16, 8, 128), f32),
-        dma(4),
+        dma(10),
     ]
-    for n in (16, 4, 8, 8, 32, 8, 1, 16, 4, 8, 8, 8, 4, 4, 4, 4, 16):
+    for n in (16, 4, 4, 2, 10, 8, 8, 32, 16, 16, 4, 8, 8, 8, 4, 4, 4, 4, 16):
         scratch += [dma(n), dma(n)]
     packed = pl.pallas_call(
         kernel,
         out_shape=jax.ShapeDtypeStruct((PACKED, 128), f32),
-        in_specs=[vmem] * 6 + [hbm] * 4,
+        in_specs=[hbm] * 10,
         out_specs=vmem,
         scratch_shapes=scratch,
         compiler_params=pltpu.CompilerParams(

time: 61.9 us -> 57.4 us (0.927)
  Pallas kernels: 61.1 us -> 56.4 us
    pallas_call x1, Pallas kernels: 59.6 us -> 54.9 us  [local(): pl.pallas_call(kernel, out_shape=jax.ShapeDtypeStruct((PACKED, 128), f32)...]
where the time goes in v3:
time: 57.4 us; the launch traced here: 57.1 us
  Pallas kernels  56.4 us (98%)
  between operations  0.64 us (1%)
    pallas_call x1, Pallas kernels, local(): pl.pallas_call(kernel, out_shape=jax.ShapeDtypeStruct((PACKED, 128), f32)...  54.9 us
    pallas_call x1, Pallas kernels, local(): pl.pallas_call(unpack, out_shape=(jax.ShapeDtypeStruct((64, 128), f32), j...  1.56 us

profile of v3, /device:TPU:1, one launch (start us, length us, event | category | flops | bytes accessed | tf_op | source)
XLA Modules:
  0.0 57.1 jit_solution(13907729679944930618)
XLA Ops:
  0.6 54.9 %ranking_backward.1.packed = f32[288,128]{1,0:T(8,128)} custom-call(bf16[1,4,1024]{2,1,0:T(4,128)(2,1)} %hist_hbm.1, f32[8,128]{1,0:T(8,128)} %bitcast.7, s32[1,64]{1,0:T(1,128)} %counts_hbm.1, s32[1,64]{1,0:T(1,128)} %slot_hbm.1, f32[1,2048]{1,0:T(1,128)} %bitcast.5, f32[1,2048]{1,0:T(1,128)} %bitcast.6, bf16[1,1024,1024]{2,1,0:T(8,128)(2,1)} %cand_hbm.1, ...), custom_call_target="tpu_custom_call" | custom-call | tf_op jit(solution)/shard_map/ranking_backward/pallas_call | solution.py:918
  55.5 1.6 %unpack.1 = (f32[64,128]{1,0:T(8,128)}, f32[64,128]{1,0:T(8,128)}, f32[64,64]{1,0:T(8,128)}, f32[16,128]{1,0:T(8,128)}, f32[16,128]{1,0:T(8,128)}, /*index=5*/f32[1,4,1024]{2,1,0:T(4,128)}) custom-call(f32[288,128]{1,0:T(8,128)} %ranking_backward.1.packed), custom_call_target="tpu_custom_call" | custom-call | tf_op jit(solution)/shard_map/unpack/pallas_call | solution.py:940

commit v4 on v3

--- a/solution.py
+++ b/solution.py
@@ -274,7 +274,10 @@
         return zh_ * 4 + x_
 
     def forward(k):
-        ahead[k] = jnp.dot(xs[...], both(wc, number(k)), preferred_element_type=f32)
+        weights = both(wc, number(k))
+        for r in range(C // HALF):
+            rows = pl.ds(r * HALF, HALF)
+            ahead[k, rows, :] = jnp.dot(xs[rows, :], weights, preferred_element_type=f32)
 
     pl.semaphore_wait(barrier, 24)
     hist_start()
@@ -693,6 +696,11 @@
     def _(j):
         u_copy(j).start()
 
+    b_second(4)
+    for k in (5, 6, 7):
+        b_second(k, (1, 2, 3))
+    a_second(1, (0, 1, 2))
+
     totals = tsend[...]
     for j in range(1, 4):
         t_copy(j).wait_recv()
@@ -700,11 +708,6 @@
     frecv[d] = totals
     f_start, f_forward, f_recv, f_send = gather(lambda i: frecv.at[i], f_s, f_r)
     f_start()
-
-    b_second(4)
-    for k in (5, 6, 7):
-        b_second(k, (1, 2, 3))
-    a_second(1, (0, 1, 2))
 
     last_stage(0)
 

time: 57.4 us -> 57 us (level)
  no operation moved by 1% of the time
where the time goes in v4:
time: 57 us; the launch traced here: 56.9 us
  Pallas kernels  56.3 us (99%)
  between operations  0.64 us (1%)
    pallas_call x1, Pallas kernels, local(): pl.pallas_call(kernel, out_shape=jax.ShapeDtypeStruct((PACKED, 128), f32)...  54.7 us
    pallas_call x1, Pallas kernels, local(): pl.pallas_call(unpack, out_shape=(jax.ShapeDtypeStruct((64, 128), f32), j...  1.56 us

profile of v4, /device:TPU:1, one launch (start us, length us, event | category | flops | bytes accessed | tf_op | source)
XLA Modules:
  0.0 56.9 jit_solution(15587281535046225415)
XLA Ops:
  0.6 54.7 %ranking_backward.1.packed = f32[288,128]{1,0:T(8,128)} custom-call(bf16[1,4,1024]{2,1,0:T(4,128)(2,1)} %hist_hbm.1, f32[8,128]{1,0:T(8,128)} %bitcast.7, s32[1,64]{1,0:T(1,128)} %counts_hbm.1, s32[1,64]{1,0:T(1,128)} %slot_hbm.1, f32[1,2048]{1,0:T(1,128)} %bitcast.5, f32[1,2048]{1,0:T(1,128)} %bitcast.6, bf16[1,1024,1024]{2,1,0:T(8,128)(2,1)} %cand_hbm.1, ...), custom_call_target="tpu_custom_call" | custom-call | tf_op jit(solution)/shard_map/ranking_backward/pallas_call | solution.py:921
  55.3 1.6 %unpack.1 = (f32[64,128]{1,0:T(8,128)}, f32[64,128]{1,0:T(8,128)}, f32[64,64]{1,0:T(8,128)}, f32[16,128]{1,0:T(8,128)}, f32[16,128]{1,0:T(8,128)}, /*index=5*/f32[1,4,1024]{2,1,0:T(4,128)}) custom-call(f32[288,128]{1,0:T(8,128)} %ranking_backward.1.packed), custom_call_target="tpu_custom_call" | custom-call | tf_op jit(solution)/shard_map/unpack/pallas_call | solution.py:943

commit v5 on v4

--- a/solution.py
+++ b/solution.py
@@ -606,9 +606,9 @@
     def _(j):
         y_msg(j).start()
 
-    a_copy(4).start()
     back(6, z2, 0)
     stage(5, True)
+    a_copy(4).start()
     a_copy(5).start()
     middle(3)
     back(7, z2, 1)

time: 57 us -> 57.1 us (level)
  no operation moved by 1% of the time
where the time goes in v5:
time: 57.1 us; the launch traced here: 56.9 us
  Pallas kernels  56.3 us (99%)
  between operations  0.64 us (1%)
    pallas_call x1, Pallas kernels, local(): pl.pallas_call(kernel, out_shape=jax.ShapeDtypeStruct((PACKED, 128), f32)...  54.7 us
    pallas_call x1, Pallas kernels, local(): pl.pallas_call(unpack, out_shape=(jax.ShapeDtypeStruct((64, 128), f32), j...  1.56 us

profile of v5, /device:TPU:1, one launch (start us, length us, event | category | flops | bytes accessed | tf_op | source)
XLA Modules:
  0.0 56.9 jit_solution(17060346517716252300)
XLA Ops:
  0.6 54.7 %ranking_backward.1.packed = f32[288,128]{1,0:T(8,128)} custom-call(bf16[1,4,1024]{2,1,0:T(4,128)(2,1)} %hist_hbm.1, f32[8,128]{1,0:T(8,128)} %bitcast.7, s32[1,64]{1,0:T(1,128)} %counts_hbm.1, s32[1,64]{1,0:T(1,128)} %slot_hbm.1, f32[1,2048]{1,0:T(1,128)} %bitcast.5, f32[1,2048]{1,0:T(1,128)} %bitcast.6, bf16[1,1024,1024]{2,1,0:T(8,128)(2,1)} %cand_hbm.1, ...), custom_call_target="tpu_custom_call" | custom-call | tf_op jit(solution)/shard_map/ranking_backward/pallas_call | solution.py:921
  55.4 1.6 %unpack.1 = (f32[64,128]{1,0:T(8,128)}, f32[64,128]{1,0:T(8,128)}, f32[64,64]{1,0:T(8,128)}, f32[16,128]{1,0:T(8,128)}, f32[16,128]{1,0:T(8,128)}, /*index=5*/f32[1,4,1024]{2,1,0:T(4,128)}) custom-call(f32[288,128]{1,0:T(8,128)} %ranking_backward.1.packed), custom_call_target="tpu_custom_call" | custom-call | tf_op jit(solution)/shard_map/unpack/pallas_call | solution.py:943
